TPU v7x, 32 devices: a whole 2x2x4 slice. The times are simulated.
32 devices in a mesh: dp: 4 (over y, core), cls: 8 (over z, x).
Axes of the slice: x: 2, y: 2, z: 4, core: 2. Of those that a mesh axis runs over, the one named last changes fastest.
Arguments:
- embeddings: bfloat16 [32768, 512], P(('dp', 'cls'))
- proxies: bfloat16 [24576, 512], P('cls')
- hard_tiles: int32 [256, 8], P(('dp', 'cls')), may hold values from 0 to 191, as said below
- tile_count: int32 [256], P(('dp', 'cls')), may hold values from 5 to 8
- labels: int32 [32768], P(('dp', 'cls')), may hold values from 0 to 24575, as said below
Outputs:
- row_loss: float32 [32768], P(('dp', 'cls'))
- embed_grad: bfloat16 [32768, 512], P(('dp', 'cls'))
- proxy_grad: float32 [24576, 512], P('cls', 'dp')
Inputs may be any that keep to these rules, and one draw needn't show every extreme that they name: `hard_tiles`: tile t is stored on class shard t // 24. Among the 8 x 8 list entries of one device's blocks (all entries, used or not), every one of the class shards is named exactly 8 times; the entries of one block name different tiles. Only the first tile_count entries of a block's list are used. `labels`: A row's positive class lies in the first tile of its block's list.
All inputs are finite; a program needn't handle non-finite values.
Results may differ from a plain program's by a relative error of at most 0.0098.
Values may be sent and summed in bfloat16 or wider, within the bound.
No kernel may reach another device: no remote copies, remote signals or barrier semaphores. Data moves between devices by JAX's collectives and lax.ppermute only.
A program may use at most 128 MiB of HBM per device.

v0:
```python
import functools

import jax
import jax.numpy as jnp
import numpy as np
from jax import lax
from jax.experimental import pallas as pl
from jax.experimental.pallas import tpu as pltpu
from jax.sharding import PartitionSpec as P

D = 512
TILE = 128
BR = 128
K = 8
PAIRS_PER_STEP = 4
FIELD = 128
PIECES = 4
VMEM_BYTES = 60 * 1024 * 1024
SPARE_BYTES = 4 * 1024 * 1024

logit_scale = 4.0
epsilon = 1e-06
unused_logit = -1e30

SMEM = pl.BlockSpec(memory_space=pltpu.SMEM)
VMEM = pl.BlockSpec(memory_space=pltpu.VMEM)
ANY = pl.BlockSpec(memory_space=pl.ANY)


def run_copies(jobs, sems, first=0):
    copies = [
        pltpu.make_async_copy(source, target, sems.at[first + index])
        for index, (source, target) in enumerate(jobs)
    ]
    for copy in copies:
        copy.start()
    return copies


def row_places(meta_ref, refs, blocks):
    size = blocks // PIECES
    if len(refs) > 1:
        return [(ref, piece * size) for piece, ref in enumerate(refs)]
    return [
        (refs[0].at[pl.ds(place * size, size)], (meta_ref[2] ^ place) * size)
        for place in range(PIECES)
    ]


def row_jobs(meta_ref, refs, rows_ref):
    return [
        (ref, rows_ref.at[pl.ds(start, ref.shape[0])])
        for ref, start in row_places(meta_ref, refs, rows_ref.shape[0])
    ]


def store_rows(meta_ref, rows_acc, out_ref, grad_refs, sems):
    blocks = out_ref.shape[0]
    out_ref[...] = rows_acc[:blocks].astype(out_ref.dtype)
    return run_copies(
        [
            (out_ref.at[pl.ds(start, ref.shape[0])], ref)
            for ref, start in row_places(meta_ref, grad_refs, blocks)
        ],
        sems,
    )


def aligned(refs, row, turned):
    parts = [ref[row] for ref in refs]
    if not turned:
        return parts
    size = parts[0].shape[0] // PIECES
    return [
        jnp.concatenate(
            [part[(piece ^ away) * size:((piece ^ away) + 1) * size] for piece in range(PIECES)]
        )
        for away, part in enumerate(parts)
    ]


def table_jobs(meta_ref, table_refs, table_ref):
    core = meta_ref[1] % 2
    jobs = [(table_refs[0], table_ref.at[pl.ds(0, table_refs[0].shape[0])])]
    if len(table_refs) > 1:
        half = table_refs[1].shape[0]
        jobs.append((table_refs[1], table_ref.at[pl.ds((2 + core) * half, half)]))
        jobs.append((table_refs[2], table_ref.at[pl.ds((3 - core) * half, half)]))
    return jobs


def transposed_logits(tile, rows):
    return logit_scale * lax.dot_general(
        tile, rows, (((1,), (1,)), ((), ())), preferred_element_type=jnp.float32
    )


def decode(code):
    return code // (2 * FIELD), (code // 2) % FIELD, (code % 2) == 1


def score_kernel(n_rows, n_tables, blocks, tiles, codes_ref, meta_ref, hit_ref, *refs):
    row_refs, refs = refs[:n_rows], refs[n_rows:]
    table_refs, refs = refs[:n_tables], refs[n_tables:]
    stats_ref, rows_ref, table_ref, lse_ref, pos_ref, sems = refs
    row_copies = run_copies(row_jobs(meta_ref, row_refs, rows_ref), sems)
    table_copies = run_copies(table_jobs(meta_ref, table_refs, table_ref), sems, PIECES)
    lse_ref[...] = jnp.full(lse_ref.shape, unused_logit, jnp.float32)
    pos_ref[...] = jnp.zeros(pos_ref.shape, jnp.float32)
    class_at = lax.broadcasted_iota(jnp.int32, (TILE, BR), 0)
    for copy in row_copies:
        copy.wait()

    def normalise(block, carry):
        exact = rows_ref[block].astype(jnp.float32)
        norm = lax.rsqrt(jnp.sum(exact * exact, axis=1, keepdims=True) + epsilon)
        rows_ref[block] = (exact * norm).astype(jnp.bfloat16)
        return carry

    lax.fori_loop(0, blocks, normalise, 0)
    for copy in table_copies:
        copy.wait()

    def step(index, carry):
        held = []
        for lane in range(PAIRS_PER_STEP):
            block, tile, first = decode(codes_ref[index * PAIRS_PER_STEP + lane])
            source = jnp.minimum(block, blocks - 1)
            logits = transposed_logits(
                table_ref[jnp.minimum(tile, tiles - 1)], rows_ref[source]
            )
            peak = jnp.max(logits, axis=0, keepdims=True)
            total = jnp.sum(jnp.exp(logits - peak), axis=0, keepdims=True)
            hit = class_at == hit_ref[pl.ds(source, 1), :]
            positive = jnp.sum(jnp.where(hit, logits, 0.0), axis=0, keepdims=True)
            held.append((block, peak + jnp.log(total), jnp.where(first, positive, 0.0)))
        for block, lse, positive in held:
            before = lse_ref[pl.ds(block, 1), :]
            top = jnp.maximum(before, lse)
            lse_ref[pl.ds(block, 1), :] = top + jnp.log(
                jnp.exp(before - top) + jnp.exp(lse - top)
            )
            pos_ref[pl.ds(block, 1), :] += positive
        return carry

    lax.fori_loop(0, pl.cdiv(meta_ref[0], PAIRS_PER_STEP), step, 0)
    stats_ref[0] = lse_ref[:blocks, :]
    stats_ref[1] = pos_ref[:blocks, :]


def make_totals(stat_refs, turned, total_ref, loss_ref):
    lse = aligned(stat_refs, 0, turned)
    top = functools.reduce(jnp.maximum, lse)
    total = top + jnp.log(sum(jnp.exp(part - top) for part in lse))
    total_ref[...] = total
    loss_ref[...] = total - sum(aligned(stat_refs, 1, turned))


def pair_score(code, blocks, tiles, rows_ref, table_ref, hit_ref, total_ref, class_at):
    block, tile, first = decode(code)
    source = jnp.minimum(block, blocks - 1)
    table_at = jnp.minimum(tile, tiles - 1)
    logits = transposed_logits(table_ref[table_at], rows_ref[source])
    share = jnp.exp(logits - total_ref[pl.ds(source, 1), :])
    wanted = jnp.where(first, hit_ref[pl.ds(source, 1), :], -1)
    hit = (class_at == wanted).astype(jnp.float32)
    return (logit_scale * (share - hit)).astype(jnp.bfloat16)


def row_terms(score, tile):
    return lax.dot_general(
        score, tile, (((0,), (0,)), ((), ())), preferred_element_type=jnp.float32
    )


def grad_kernel(
    n_grads, n_tables, n_stats, turned, blocks, tiles, codes_ref, meta_ref, hit_ref, *refs
):
    stat_refs, refs = refs[:n_stats], refs[n_stats:]
    unit_ref, refs = refs[0], refs[1:]
    table_refs, refs = refs[:n_tables], refs[n_tables:]
    grad_refs, refs = refs[:n_grads], refs[n_grads:]
    scores_ref, loss_ref, rows_ref, table_ref, total_ref, rows_acc, out_ref, sems = refs
    copies = run_copies(
        [(unit_ref, rows_ref)] + table_jobs(meta_ref, table_refs, table_ref), sems, PIECES
    )
    rows_acc[...] = jnp.zeros(rows_acc.shape, jnp.float32)
    make_totals(stat_refs, turned, total_ref, loss_ref)
    class_at = lax.broadcasted_iota(jnp.int32, (TILE, BR), 0)
    for copy in copies:
        copy.wait()

    def step(index, carry):
        held = []
        for lane in range(PAIRS_PER_STEP):
            pair = index * PAIRS_PER_STEP + lane
            score = pair_score(
                codes_ref[pair], blocks, tiles, rows_ref, table_ref, hit_ref, total_ref, class_at
            )
            scores_ref[pair] = score
            held.append(score)
        for lane, score in enumerate(held):
            block, tile, _ = decode(codes_ref[index * PAIRS_PER_STEP + lane])
            rows_acc[block] += row_terms(score, table_ref[jnp.minimum(tile, tiles - 1)])
        return carry

    lax.fori_loop(0, pl.cdiv(meta_ref[0], PAIRS_PER_STEP), step, 0)
    for copy in store_rows(meta_ref, rows_acc, out_ref, grad_refs, sems):
        copy.wait()


def last_kernel(sizes, n_grads, n_tables, n_stats, turned, n_shares, tiles, *refs):
    chunks, blocks = len(sizes), sizes[-1]
    codes_refs, refs = refs[:chunks], refs[chunks:]
    meta_refs, refs = refs[:chunks], refs[chunks:]
    hit_ref, refs = refs[0], refs[1:]
    stat_refs, refs = refs[:n_stats], refs[n_stats:]
    scores_refs, refs = refs[:chunks - 1], refs[chunks - 1:]
    unit_refs, refs = refs[:chunks], refs[chunks:]
    table_refs, refs = refs[:n_tables], refs[n_tables:]
    grad_refs, refs = refs[:n_grads], refs[n_grads:]
    share_refs, refs = refs[:n_shares], refs[n_shares:]
    loss_ref, refs = refs[0], refs[1:]
    rows_ref, early_ref, held_ref, table_ref, total_ref, rows_acc, out_ref, *refs = refs
    tiles_acc, sems, early_sems, row_sems = refs
    codes_ref, meta_ref = codes_refs[-1], meta_refs[-1]
    copies = run_copies(
        [(unit_refs[-1], rows_ref)] + table_jobs(meta_ref, table_refs, table_ref), sems
    )


    def fetch(chunk):
        early = early_ref.at[pl.ds(0, sizes[chunk])]
        return run_copies(
            [(unit_refs[chunk], early), (scores_refs[chunk], held_ref)], early_sems
        )

    early = fetch(0) if chunks > 1 else []
    rows_acc[...] = jnp.zeros(rows_acc.shape, jnp.float32)
    tiles_acc[...] = jnp.zeros(tiles_acc.shape, jnp.float32)
    make_totals(stat_refs, turned, total_ref, loss_ref)
    class_at = lax.broadcasted_iota(jnp.int32, (TILE, BR), 0)
    for copy in copies:
        copy.wait()

    def step(index, carry):
        held = [
            pair_score(
                codes_ref[index * PAIRS_PER_STEP + lane], blocks, tiles, rows_ref, table_ref,
                hit_ref, total_ref, class_at,
            )
            for lane in range(PAIRS_PER_STEP)
        ]
        for lane, score in enumerate(held):
            block, tile, _ = decode(codes_ref[index * PAIRS_PER_STEP + lane])
            rows_acc[block] += row_terms(score, table_ref[jnp.minimum(tile, tiles - 1)])
            tiles_acc[tile] += jnp.dot(
                score, rows_ref[jnp.minimum(block, blocks - 1)],
                preferred_element_type=jnp.float32,
            )
        return carry

    lax.fori_loop(0, pl.cdiv(meta_ref[0], PAIRS_PER_STEP), step, 0)
    stored = store_rows(meta_ref, rows_acc, out_ref, grad_refs, row_sems)
    for chunk in range(chunks - 1):
        for copy in early if chunk == 0 else fetch(chunk):
            copy.wait()

        def early_step(index, carry, chunk=chunk):
            for lane in range(PAIRS_PER_STEP):
                pair = index * PAIRS_PER_STEP + lane
                block, tile, _ = decode(codes_refs[chunk][pair])
                tiles_acc[tile] += jnp.dot(
                    held_ref[pair],
                    early_ref[jnp.minimum(block, sizes[chunk] - 1)],
                    preferred_element_type=jnp.float32,
                )
            return carry

        lax.fori_loop(0, pl.cdiv(meta_refs[chunk][0], PAIRS_PER_STEP), early_step, 0)
    if n_shares == 1:
        share_refs[0][...] = tiles_acc[:tiles].astype(jnp.bfloat16)
    else:
        part = meta_ref[1]
        shard, width = share_refs[0].shape[2], share_refs[0].shape[-1]
        for core, ref in enumerate(share_refs):
            for y in range(ref.shape[1]):
                start = pl.multiple_of(((2 * y + core) ^ part) * width, width)
                for x in range(ref.shape[0]):
                    ref[x, y] = tiles_acc[
                        pl.ds(x * shard, shard), :, pl.ds(start, width)
                    ].astype(jnp.bfloat16)
    for copy in stored:
        copy.wait()


def kernel_cost(blocks):
    return pl.CostEstimate(flops=blocks * BR * D, bytes_accessed=blocks * BR * D, transcendentals=0)


def limit(*scratch):
    total = 0
    for shape, dtype in scratch:
        total += int(np.prod(shape)) * jnp.dtype(dtype).itemsize
    return pltpu.CompilerParams(vmem_limit_bytes=min(VMEM_BYTES, total + SPARE_BYTES))


def rows_of(blocks):
    return (blocks, BR, D), jnp.bfloat16


def score(blocks, codes, meta, hit, rows, tables):
    tiles = sum(table.shape[0] for table in tables)
    table_room = ((tiles, TILE, D), jnp.bfloat16)
    return pl.pallas_call(
        functools.partial(score_kernel, len(rows), len(tables), blocks, tiles),
        out_shape=(
            jax.ShapeDtypeStruct((2, blocks, BR), jnp.float32),
            jax.ShapeDtypeStruct(*rows_of(blocks)),
        ),
        in_specs=[SMEM, SMEM, VMEM] + [ANY] * (len(rows) + len(tables)),
        out_specs=(VMEM, VMEM),
        scratch_shapes=[
            pltpu.VMEM(*table_room),
            pltpu.VMEM((blocks + 8, BR), jnp.float32),
            pltpu.VMEM((blocks + 8, BR), jnp.float32),
            pltpu.SemaphoreType.DMA((PIECES + len(tables),)),
        ],
        cost_estimate=kernel_cost(blocks),
        compiler_params=limit(rows_of(blocks), table_room),
    )(codes, meta, hit, *rows, *tables)


def grads(blocks, codes, meta, hit, stats, turned, unit, tables, shapes):
    tiles = sum(table.shape[0] for table in tables)
    table_room = ((tiles, TILE, D), jnp.bfloat16)
    acc_room = ((blocks + 1, BR, D), jnp.float32)
    scores = ((codes.shape[0], TILE, BR), jnp.bfloat16)
    outs = pl.pallas_call(
        functools.partial(
            grad_kernel, len(shapes), len(tables), len(stats), turned, blocks, tiles
        ),
        out_shape=(
            *(jax.ShapeDtypeStruct(shape, jnp.bfloat16) for shape in shapes),
            jax.ShapeDtypeStruct(*scores),
            jax.ShapeDtypeStruct((blocks, BR), jnp.float32),
        ),
        in_specs=[SMEM, SMEM] + [VMEM] * (1 + len(stats)) + [ANY] * (1 + len(tables)),
        out_specs=(*[ANY] * len(shapes), VMEM, VMEM),
        scratch_shapes=[
            pltpu.VMEM(*rows_of(blocks)),
            pltpu.VMEM(*table_room),
            pltpu.VMEM((blocks, BR), jnp.float32),
            pltpu.VMEM(*acc_room),
            pltpu.VMEM(*rows_of(blocks)),
            pltpu.SemaphoreType.DMA((PIECES + 1 + len(tables),)),
        ],
        cost_estimate=kernel_cost(blocks),
        compiler_params=limit(rows_of(2 * blocks), table_room, acc_room, scores),
    )(codes, meta, hit, *stats, unit, *tables)
    return list(outs[:len(shapes)]), outs[len(shapes)], outs[-1]


def last_grads(codes, metas, hit, stats, turned, scores, units, tables, shapes, share_shapes):
    sizes = [unit.shape[0] for unit in units]
    tiles = sum(table.shape[0] for table in tables)
    chunks, blocks = len(sizes), sizes[-1]
    n_inputs = 2 * chunks - 1 + len(tables)
    table_room = ((tiles, TILE, D), jnp.bfloat16)
    acc_room = ((blocks + 1, BR, D), jnp.float32)
    tiles_room = ((tiles + 1, TILE, D), jnp.float32)
    early_room = rows_of(max(sizes[:-1], default=PIECES))
    kept = ((scores or codes)[0].shape[0], TILE, BR), jnp.bfloat16
    outs = pl.pallas_call(
        functools.partial(
            last_kernel, sizes, len(shapes), len(tables), len(stats), turned,
            len(share_shapes), tiles,
        ),
        out_shape=(
            *(jax.ShapeDtypeStruct(shape, jnp.bfloat16) for shape in shapes),
            *(jax.ShapeDtypeStruct(shape, jnp.bfloat16) for shape in share_shapes),
            jax.ShapeDtypeStruct((blocks, BR), jnp.float32),
        ),
        in_specs=[SMEM] * (2 * chunks) + [VMEM] * (1 + len(stats)) + [ANY] * n_inputs,
        out_specs=(*[ANY] * len(shapes), *[VMEM] * len(share_shapes), VMEM),
        scratch_shapes=[
            pltpu.VMEM(*rows_of(blocks)),
            pltpu.VMEM(*early_room),
            pltpu.VMEM(*kept),
            pltpu.VMEM(*table_room),
            pltpu.VMEM((blocks, BR), jnp.float32),
            pltpu.VMEM(*acc_room),
            pltpu.VMEM(*rows_of(blocks)),
            pltpu.VMEM(*tiles_room),
            pltpu.SemaphoreType.DMA((1 + len(tables),)),
            pltpu.SemaphoreType.DMA((2,)),
            pltpu.SemaphoreType.DMA((PIECES,)),
        ],
        cost_estimate=kernel_cost(sum(sizes)),
        compiler_params=limit(
            rows_of(2 * blocks), early_room, kept, table_room, table_room, acc_room, tiles_room
        ),
    )(*codes, *metas, hit, *stats, *scores, *units, *tables)
    cut = len(shapes)
    return list(outs[:cut]), list(outs[cut:-1]), outs[-1]


def add(first, second):
    return (first.astype(jnp.float32) + second.astype(jnp.float32)).astype(jnp.bfloat16)


class Neighbours:
    def __init__(self, nx, dp):
        self.nx, self.nz, self.dp, self.turned = nx, PIECES, dp, True

    def over_z(self, value, away):
        pairs = [
            (z * self.nx + x, (z ^ away) * self.nx + x)
            for z in range(self.nz) for x in range(self.nx)
        ]
        return lax.ppermute(value, "cls", pairs)

    def over_x(self, value):
        return lax.ppermute(value, "cls", [(c, c ^ 1) for c in range(self.nx * self.nz)])

    def over_y(self, value):
        return lax.ppermute(value, "dp", [(d, d ^ 2) for d in range(self.dp)])

    def over_core(self, value):
        return lax.ppermute(value, "dp", [(d, d ^ 1) for d in range(self.dp)])

    def all_over_z(self, value):
        return [value] + [self.over_z(value, away) for away in range(1, self.nz)]

    def gather(self, needed, chunks, lists, table, core, prepare):
        def moves(first, lists, table, core):
            half = table.shape[0] // 2
            sent = lax.dynamic_slice_in_dim(table, core * half, half, axis=0)
            far, near, from_x = lax.optimization_barrier(
                (self.over_z(first, 2), self.over_z(first, 1), self.over_x(sent))
            )
            return (near, far, self.over_z(far, 1)), (from_x, self.over_core(from_x)), prepare(
                jnp.stack(self.all_over_z(lists))
            )

        first, second = chunks
        pieces, tables, prepared = self.together(needed, moves, first, lists, table, core)
        return [[first, *pieces], [second]], [table, *tables], prepared

    def rest_of_rows(self, pieces, others):
        second, = pieces
        far, near, others = lax.optimization_barrier(
            (self.over_z(second, 2), self.over_z(second, 1), others)
        )
        return (near, far, self.over_z(far, 1)), others

    def whole_rows(self, pieces, rest):
        return [*pieces, *rest]

    def grad_shapes(self, size):
        return [(size, BR, D)] * PIECES

    def gather_stats(self, stats):
        return self.all_over_z(stats)

    def order(self, place):
        return place

    def own(self, loss, place, size):
        return loss[:size]

    def early_return(self, early, others):
        parts, = early
        near, passed = self.over_z(parts[1], 1), self.over_z(parts[3], 1)
        passed, others = lax.optimization_barrier((passed, others))
        return (near, self.over_z(add(passed, parts[2]), 2)), others

    def early_sums(self, early, returned):
        return [sum(part.astype(jnp.float32) for part in (early[0][0], *returned))]

    def together(self, needed, work, *operands):
        def no_work(*operands):
            return jax.tree.map(
                lambda out: jnp.zeros(out.shape, out.dtype), jax.eval_shape(work, *operands)
            )

        return lax.cond(needed, work, no_work, *operands)

    def sum_last(self, parts, shares):
        kept, sent = shares
        passed, got = self.over_z(parts[3], 1), self.over_core(sent)
        near = self.over_z(parts[1], 1)
        half = kept.shape[2] // 2
        x_sent = add(kept[1, :, :half], got[1, :, :half])
        y_sent = add(kept[:, 1, half:], got[:, 1, half:])
        passed, _, _ = lax.optimization_barrier((passed, x_sent, y_sent))
        far = self.over_z(add(passed, parts[2]), 2)
        total = sum(part.astype(jnp.float32) for part in (parts[0], near, far))
        return total, self.sum_shares(kept, got, x_sent, y_sent)

    def share_shapes(self, shard_tiles):
        return [(self.nx, self.dp // 2, shard_tiles, TILE, D // self.dp)] * 2

    def sum_shares(self, kept, got, x_sent, y_sent):
        half = kept.shape[2] // 2
        x_got, y_got = lax.optimization_barrier((self.over_x(x_sent), self.over_y(y_sent)))
        x_kept = [add(add(kept[0, y, :half], got[0, y, :half]), x_got[y]) for y in range(2)]
        y_kept = [add(add(kept[x, 0, half:], got[x, 0, half:]), y_got[x]) for x in range(2)]
        low, high = lax.optimization_barrier((self.over_y(x_kept[1]), self.over_x(y_kept[1])))
        low = x_kept[0].astype(jnp.float32) + low.astype(jnp.float32)
        high = y_kept[0].astype(jnp.float32) + high.astype(jnp.float32)
        return jnp.concatenate([low, high], axis=0)


class Groups:
    def __init__(self, nz, dp):
        self.nx, self.nz, self.dp, self.turned = 1, nz, dp, False

    def gather(self, needed, chunks, lists, table, core, prepare):
        gathered = [[lax.all_gather(rows, "cls", tiled=True)] for rows in chunks]
        return gathered, [table], prepare(lax.all_gather(lists, "cls"))

    def rest_of_rows(self, pieces, others):
        return (), others

    def whole_rows(self, pieces, rest):
        return pieces

    def grad_shapes(self, size):
        return [(self.nz * size, BR, D)]

    def gather_stats(self, stats):
        return list(lax.all_gather(stats, "cls"))

    def order(self, place):
        return jnp.zeros_like(place)

    def own(self, loss, place, size):
        return lax.dynamic_slice_in_dim(loss, place * size, size, axis=0)

    def total(self, part):
        return lax.psum_scatter(
            part, "cls", scatter_dimension=0, tiled=True
        ).astype(jnp.float32)

    def early_return(self, early, others):
        return [self.total(part) for part, in early], others

    def early_sums(self, early, returned):
        return returned

    def together(self, needed, work, *operands):
        return work(*operands)

    def sum_last(self, parts, shares):
        return self.total(parts[0]), self.sum_shares(shares)

    def share_shapes(self, shard_tiles):
        return [(shard_tiles, TILE, D)]

    def sum_shares(self, shares):
        return lax.psum_scatter(
            shares[0], "dp", scatter_dimension=2, tiled=True
        ).astype(jnp.float32)


def pair_codes(lists, shard_tiles, nx, place, column, room):
    entry = lists[:, :K].reshape(-1)
    owner = entry // shard_tiles
    mine = (entry >= 0) & (owner // nx == place)
    local = jnp.where(owner % nx == column, 0, shard_tiles) + entry % shard_tiles
    counter = jnp.arange(entry.shape[0], dtype=jnp.int32)
    code = ((counter // K) * FIELD + local) * 2 + (counter % K == 0)
    rank = jnp.sum(
        jnp.where(mine[None, :] & (counter[None, :] < counter[:, None]), 1, 0), axis=1
    ).astype(jnp.int32)
    slots = jnp.arange(room, dtype=jnp.int32)
    chosen = mine[None, :] & (rank[None, :] == slots[:, None])
    padding = (lists.shape[0] * FIELD + nx * shard_tiles) * 2
    codes = padding + jnp.sum(jnp.where(chosen, code[None, :] - padding, 0), axis=1)
    return codes.astype(jnp.int32), jnp.sum(mine.astype(jnp.int32))


def per_device(moves, sizes, embeddings, proxies, hard_tiles, tile_count, labels):
    nx, nz, dp = moves.nx, moves.nz, moves.dp
    blocks = hard_tiles.shape[0]
    shard_tiles = proxies.shape[0] // TILE
    me, part = lax.axis_index("cls"), lax.axis_index("dp")
    place, column = me // nx, me % nx

    row_blocks = embeddings.reshape(blocks, BR, D)

    position = labels.reshape(blocks, BR) - hard_tiles[:, 0:1] * TILE
    entries = jnp.arange(K, dtype=jnp.int32)
    used = jnp.where(entries[None, :] < tile_count[:, None], hard_tiles, -1)
    starts = [sum(sizes[:chunk]) for chunk in range(len(sizes))]
    spots = [slice(start, start + size) for start, size in zip(starts, sizes)]
    held = [nz * size for size in sizes]
    last = len(sizes) - 1
    needed = tile_count[0] > 0

    def prepare(lists):
        prepared = []
        for spot, blocks_held in zip(spots, held):
            room = min(blocks_held * K, nz * (blocks * K // (nx * nz)) * nx)
            room = -(-room // PAIRS_PER_STEP) * PAIRS_PER_STEP
            chunk_lists = lists[:, spot].reshape(blocks_held, K + BR)
            code, count = pair_codes(chunk_lists, shard_tiles, nx, place, column, room)
            meta = jnp.stack([count, part, moves.order(place)]).astype(jnp.int32)
            prepared.append((code, meta, chunk_lists[:, K:]))
        return prepared

    gathered, tables, prepared = moves.gather(
        needed,
        [row_blocks[spot] for spot in spots],
        jnp.concatenate([used, position], axis=1),
        proxies.reshape(shard_tiles, TILE, D),
        part % 2,
        prepare,
    )

    def scored(chunk, rows, tables, prepared):
        parts, unit = score(held[chunk], *prepared[chunk], rows, tables)
        return moves.gather_stats(parts), unit

    def early_work(gathered, tables, prepared):
        units, made, rest = [], [], ()
        for chunk in range(last):
            stats, unit = scored(chunk, gathered[chunk], tables, prepared)
            if chunk == 0:
                rest, stats = moves.rest_of_rows(gathered[-1], stats)
            units.append(unit)
            made.append(grads(
                held[chunk], *prepared[chunk], stats, moves.turned, unit, tables,
                moves.grad_shapes(sizes[chunk]),
            ))
        return rest, units, made

    def last_work(rows, tables, prepared, units, scores, early):
        codes, metas, hits = zip(*prepared)
        stats, unit = scored(last, rows, tables, prepared)
        returned, stats = moves.early_return(early, stats)
        return returned, last_grads(
            codes, metas, hits[-1], stats, moves.turned, scores, units + [unit], tables,
            moves.grad_shapes(sizes[-1]), moves.share_shapes(shard_tiles),
        )

    rest, units, made = moves.together(needed, early_work, gathered, tables, prepared)
    rows = moves.whole_rows(gathered[-1], rest)
    early, scores, losses = zip(*made)
    returned, (parts, shares, loss) = moves.together(
        needed, last_work, rows, tables, prepared, units, list(scores), early
    )
    total, shares = moves.sum_last(parts, shares)
    row_grads = moves.early_sums(early, returned) + [total]
    losses = [
        moves.own(part, place, size) for part, size in zip((*losses, loss), sizes)
    ]

    embeddings, units = lax.optimization_barrier((embeddings, units))
    emb_exact = embeddings.astype(jnp.float32)
    inverse_norm = lax.rsqrt(jnp.sum(emb_exact * emb_exact, axis=1, keepdims=True) + epsilon)
    unit_exact = emb_exact * inverse_norm
    proxy_grad = shares.reshape(shard_tiles * TILE, D // dp)
    row_loss = jnp.concatenate(losses, axis=0).reshape(-1)
    grad_flat = jnp.concatenate(row_grads, axis=0)
    grad_flat = grad_flat.reshape(blocks * BR, D)
    radial = jnp.sum(unit_exact * grad_flat, axis=1, keepdims=True)
    embed_grad = ((grad_flat - unit_exact * radial) * inverse_norm).astype(jnp.bfloat16)
    return (row_loss, embed_grad, proxy_grad)


def solution(mesh):
    placed = (
        P(("dp", "cls"), None),
        P("cls", None),
        P(("dp", "cls"), None),
        P(("dp", "cls")),
        P(("dp", "cls")),
    )
    dp, groups = mesh.shape["dp"], mesh.shape["cls"]
    if (dp, groups) == (4, 2 * PIECES):
        moves, sizes = Neighbours(2, dp), [4, 4]
    else:
        chunks = max(1, groups // 8)
        moves, sizes = Groups(groups, dp), [8 // chunks] * chunks
    return jax.shard_map(
        functools.partial(per_device, moves, sizes),
        mesh=mesh,
        in_specs=placed,
        out_specs=(P(("dp", "cls")), P(("dp", "cls"), None), P("cls", "dp")),
        check_vma=False,
    )
```

profile of v0, /device:TPU:0, one launch (start us, length us, event | category | flops | bytes accessed | tf_op | source)
XLA Modules:
  0.0 194.8 jit_solution(2182523221408652393)
XLA Ops:
  2.4 54.4 %conditional.3 = (bf16[4,128,512]{2,1,0:T(8,128)(2,1)}, bf16[4,128,512]{2,1,0:T(8,128)(2,1)}, bf16[4,128,512]{2,1,0:T(8,128)(2,1)}, bf16[12,128,512]{2,1,0:T(8,1...) conditional(s32[]{:T(128)} %bitcast.8, () %tuple.75, ...), branch_computations={%region_0.1_spmd, %region_1.8_spmd} | conditional | flops 232492 | bytes 22230328 | solution.py:487
  4.0 3.0 %collective-permute-start.14 = (bf16[12,128,512]{2,1,0:T(8,128)(2,1)S(1)}, bf16[12,128,512]{2,1,0:T(8,128)(2,1)}, u32[]{:S(2)}, u32[]{:S(2)}) collective-permute-start(bf16[12,128,512]{2,1,0:T(8,128)(2,1)S(1)} %constant_dynamic-slice_fusion), channel_id=1, source_target_pairs={{0,1},{1,0},{2,3},{3,2},{4,5},{5,4},{6,7},{7,6},{8,9},{9,8},{10,11... | collective-permute-start | bytes 4718600 | tf_op jit(solution)/shard_map/cond/branch_1_fun/ppermute | solution.py:424
  8.5 2.6 %collective-permute-start.18 = (s32[8,136]{1,0:T(8,128)S(1)}, s32[8,136]{1,0:T(8,128)S(1)}, u32[]{:S(2)}, u32[]{:S(2)}) collective-permute-start(s32[8,136]{1,0:T(8,128)S(1)} %get-tuple-element.148), channel_id=1, source_target_pairs={{0,4},{1,5},{2,6},{3,7},{4,0},{5,1},{6,2},{7,3},{8,12},{9,13},{10,... | collective-permute-start | bytes 13064 | tf_op jit(solution)/shard_map/cond/branch_1_fun/ppermute | solution.py:421
  19.1 17.4 %collective-permute-done.12 = bf16[4,128,512]{2,1,0:T(8,128)(2,1)} collective-permute-done((bf16[4,128,512]{2,1,0:T(8,128)(2,1)S(1)}, bf16[4,128,512]{2,1,0:T(8,128)(2,1)}, u32[]{:S(2)}, u32[]{:S(2)}) %collective-permute-start.12) | collective-permute-done | bytes 524320 | tf_op jit(solution)/shard_map/cond/branch_1_fun/ppermute | solution.py:421
  36.5 5.0 %collective-permute-done.14 = bf16[12,128,512]{2,1,0:T(8,128)(2,1)} collective-permute-done((bf16[12,128,512]{2,1,0:T(8,128)(2,1)S(1)}, bf16[12,128,512]{2,1,0:T(8,128)(2,1)}, u32[]{:S(2)}, u32[]{:S(2)}) %collective-permute-start.14) | collective-permute-done | bytes 1572896 | tf_op jit(solution)/shard_map/cond/branch_1_fun/ppermute | solution.py:424
  44.5 12.3 %collective-permute-done.15 = bf16[4,128,512]{2,1,0:T(8,128)(2,1)} collective-permute-done((bf16[4,128,512]{2,1,0:T(8,128)(2,1)}, bf16[4,128,512]{2,1,0:T(8,128)(2,1)}, u32[]{:S(2)}, u32[]{:S(2)}) %collective-permute-start.15) | collective-permute-done | bytes 524320 | tf_op jit(solution)/shard_map/cond/branch_1_fun/ppermute | solution.py:421
  56.8 40.7 %conditional.4 = (bf16[4,128,512]{2,1,0:T(8,128)(2,1)}, bf16[4,128,512]{2,1,0:T(8,128)(2,1)}, bf16[4,128,512]{2,1,0:T(8,128)(2,1)}, bf16[16,128,512]{2,1,0:T(8,1...) conditional(s32[]{:T(128)} %bitcast.8, () %tuple.74, ...), branch_computations={%region_8.9_spmd, %region_9.10_spmd} | conditional | flops 2359296 | bytes 22745436 | solution.py:487
  56.8 2.8 %collective-permute-start = (bf16[4,128,512]{2,1,0:T(8,128)(2,1)S(1)}, bf16[4,128,512]{2,1,0:T(8,128)(2,1)}, u32[]{:S(2)}, u32[]{:S(2)}) collective-permute-start(bf16[4,128,512]{2,1,0:T(8,128)(2,1)S(1)} %get-tuple-element.151), channel_id=1, source_target_pairs={{0,4},{1,5},{2,6},{3,7},{4,0},{5,1},{6,2},{7,3},{8,12},{9,13},{10,... | collective-permute-start | bytes 1572872 | tf_op jit(solution)/shard_map/cond/branch_1_fun/ppermute | solution.py:421
  61.1 8.7 %branch_1_fun.4 = (f32[2,16,128]{2,1,0:T(8,128)S(1)}, bf16[16,128,512]{2,1,0:T(8,128)(2,1)}) custom-call(s32[64]{0:T(128)S(1)} %get-tuple-element.152.codes_ref, s32[3]{0:T(128)S(1)} %get-tuple-element.153.meta_ref, s32[16,128]{1,0:T(8,128)S(1)} %get-tuple-element.154.hit_ref, bf16[4,128,512]{2,1,0:T(8,128)(2,1)S(1)} %get-tuple-element.155.refs_0_, ...), custom_call_target="tpu_custom_call" | custom-call | flops 1048576 | bytes 1048576 | tf_op jit(solution)/shard_map/cond/branch_1_fun/pallas_call | solution.py:315
  71.1 3.2 %collective-permute-start.4 = (f32[2,16,128]{2,1,0:T(8,128)S(1)}, f32[2,16,128]{2,1,0:T(8,128)S(1)}, u32[]{:S(2)}, u32[]{:S(2)}) collective-permute-start(f32[2,16,128]{2,1,0:T(8,128)S(1)} %get-tuple-element.166.refs_0_), channel_id=1, source_target_pairs={{0,6},{1,7},{2,4},{3,5},{4,2},{5,3},{6,0},{7,1},{8,14},{9,15},{10,... | collective-permute-start | bytes 49160 | tf_op jit(solution)/shard_map/cond/branch_1_fun/ppermute | solution.py:421
  74.3 9.5 %collective-permute-done.2.refs_1_ = f32[2,16,128]{2,1,0:T(8,128)S(1)} collective-permute-done((f32[2,16,128]{2,1,0:T(8,128)S(1)}, f32[2,16,128]{2,1,0:T(8,128)S(1)}, u32[]{:S(2)}, u32[]{:S(2)}) %collective-permute-start.2) | collective-permute-done | bytes 16416 | tf_op jit(solution)/shard_map/cond/branch_1_fun/ppermute | solution.py:421
  85.2 8.7 %branch_1_fun.5 = (bf16[4,128,512]{2,1,0:T(8,128)(2,1)S(1)}, bf16[4,128,512]{2,1,0:T(8,128)(2,1)}, bf16[4,128,512]{2,1,0:T(8,128)(2,1)S(1)}, bf16[4,128,512]{2,1...) custom-call(s32[64]{0:T(128)S(1)} %get-tuple-element.152.codes_ref, ...), custom_call_target="tpu_custom_call" | custom-call | flops 1048576 | bytes 1048576 | tf_op jit(solution)/shard_map/cond/branch_1_fun/pallas_call | solution.py:339
  94.0 3.5 %collective-permute-done.5 = bf16[4,128,512]{2,1,0:T(8,128)(2,1)} collective-permute-done((bf16[4,128,512]{2,1,0:T(8,128)(2,1)}, bf16[4,128,512]{2,1,0:T(8,128)(2,1)}, u32[]{:S(2)}, u32[]{:S(2)}) %collective-permute-start.5) | collective-permute-done | bytes 524320 | tf_op jit(solution)/shard_map/cond/branch_1_fun/ppermute | solution.py:421
  98.5 41.9 %conditional.5 = (bf16[4,128,512]{2,1,0:T(8,128)(2,1)}, bf16[4,128,512]{2,1,0:T(8,128)(2,1)}, bf16[2,2,24,128,128]{4,3,2,1,0:T(8,128)(2,1)S(1)}, bf16[2,2,24,128...) conditional(s32[]{:T(128)} %bitcast.8, () %tuple.78, ...), branch_computations={%region_10.11_spmd, %region_11.12_spmd} | conditional | flops 5242880 | bytes 30085460 | solution.py:487
  99.5 6.7 %branch_1_fun.6 = (f32[2,16,128]{2,1,0:T(8,128)S(1)}, bf16[16,128,512]{2,1,0:T(8,128)(2,1)S(1)}) custom-call(s32[64]{0:T(128)S(1)} %get-tuple-element.177.codes_ref.refs_1_, s32[3]{0:T(128)S(1)} %get-tuple-element.179.meta_ref.refs_3_, s32[16,128]{1,0:T(8,128)S(1)} %get-tuple-element.180.hit_ref.refs_4_, bf16[4,128,512]{2,1,0:T(8,128)(2,1)} %get-tuple-element.182.refs_0_, ...), custom_call_target="tpu_custom_call" | custom-call | flops 1048576 | bytes 1048576 | tf_op jit(solution)/shard_map/cond/branch_1_fun/pallas_call | solution.py:315
  107.6 3.7 %collective-permute-start.8 = (f32[2,16,128]{2,1,0:T(8,128)S(1)}, f32[2,16,128]{2,1,0:T(8,128)S(1)}, u32[]{:S(2)}, u32[]{:S(2)}) collective-permute-start(f32[2,16,128]{2,1,0:T(8,128)S(1)} %get-tuple-element.190.refs_5_), channel_id=1, source_target_pairs={{0,4},{1,5},{2,6},{3,7},{4,0},{5,1},{6,2},{7,3},{8,12},{9,13},{10,... | collective-permute-start | bytes 49160 | tf_op jit(solution)/shard_map/cond/branch_1_fun/ppermute | solution.py:421
  113.2 3.9 %collective-permute-done.9.refs_8_ = f32[2,16,128]{2,1,0:T(8,128)S(1)} collective-permute-done((f32[2,16,128]{2,1,0:T(8,128)S(1)}, f32[2,16,128]{2,1,0:T(8,128)S(1)}, u32[]{:S(2)}, u32[]{:S(2)}) %collective-permute-start.9) | collective-permute-done | bytes 16416 | tf_op jit(solution)/shard_map/cond/branch_1_fun/ppermute | solution.py:421
  117.3 13.0 %branch_1_fun.7 = (bf16[4,128,512]{2,1,0:T(8,128)(2,1)S(1)}, bf16[4,128,512]{2,1,0:T(8,128)(2,1)}, bf16[4,128,512]{2,1,0:T(8,128)(2,1)S(1)}, bf16[4,128,512]{2,1...) custom-call(s32[64]{0:T(128)S(1)} %get-tuple-element.176.refs_0_, ...), custom_call_target="tpu_custom_call" | custom-call | flops 2097152 | bytes 2097152 | tf_op jit(solution)/shard_map/cond/branch_1_fun/pallas_call | solution.py:374
  132.9 7.2 %collective-permute-done.11 = bf16[4,128,512]{2,1,0:T(8,128)(2,1)S(1)} collective-permute-done((bf16[4,128,512]{2,1,0:T(8,128)(2,1)S(1)}, bf16[4,128,512]{2,1,0:T(8,128)(2,1)S(1)}, u32[]{:S(2)}, u32[]{:S(2)}) %collective-permute-start.11) | collective-permute-done | bytes 524320 | tf_op jit(solution)/shard_map/cond/branch_1_fun/ppermute | solution.py:421
  143.5 2.9 %collective-permute-done.22 = bf16[2,2,24,128,128]{4,3,2,1,0:T(8,128)(2,1)S(1)} collective-permute-done((bf16[2,2,24,128,128]{4,3,2,1,0:T(8,128)(2,1)}, bf16[2,2,24,128,128]{4,3,2,1,0:T(8,128)(2,1)S(1)}, u32[]{:S(2)}, u32[]{:S(2)}) %collective-permute-start.22) | collective-permute-done | bytes 3145760 | tf_op jit(solution)/shard_map/ppermute | solution.py:430
  147.0 8.5 %collective-permute-done.21 = bf16[4,128,512]{2,1,0:T(8,128)(2,1)S(1)} collective-permute-done((bf16[4,128,512]{2,1,0:T(8,128)(2,1)}, bf16[4,128,512]{2,1,0:T(8,128)(2,1)S(1)}, u32[]{:S(2)}, u32[]{:S(2)}) %collective-permute-start.21) | collective-permute-done | bytes 524320 | tf_op jit(solution)/shard_map/ppermute | solution.py:421
  158.7 14.5 %collective-permute-done.20 = bf16[4,128,512]{2,1,0:T(8,128)(2,1)S(1)} collective-permute-done((bf16[4,128,512]{2,1,0:T(8,128)(2,1)}, bf16[4,128,512]{2,1,0:T(8,128)(2,1)S(1)}, u32[]{:S(2)}, u32[]{:S(2)}) %collective-permute-start.20) | collective-permute-done | bytes 524320 | tf_op jit(solution)/shard_map/ppermute | solution.py:421
  173.2 7.8 %collective-permute-done.23 = bf16[4,128,512]{2,1,0:T(8,128)(2,1)S(1)} collective-permute-done((bf16[4,128,512]{2,1,0:T(8,128)(2,1)S(1)}, bf16[4,128,512]{2,1,0:T(8,128)(2,1)S(1)}, u32[]{:S(2)}, u32[]{:S(2)}) %collective-permute-start.23) | collective-permute-done | bytes 524320 | tf_op jit(solution)/shard_map/ppermute | solution.py:421
  186.5 5.1 %collective-permute-done.26 = bf16[12,128,128]{2,1,0:T(8,128)(2,1)S(1)} collective-permute-done((bf16[12,128,128]{2,1,0:T(8,128)(2,1)S(1)}, bf16[12,128,128]{2,1,0:T(8,128)(2,1)S(1)}, u32[]{:S(2)}, u32[]{:S(2)}) %collective-permute-start.26) | collective-permute-done | bytes 393248 | tf_op jit(solution)/shard_map/ppermute | solution.py:427
  (120 shorter events, 43.9 us)
Async XLA Ops:
  4.0 37.5 %collective-permute-start.14 = (bf16[12,128,512]{2,1,0:T(8,128)(2,1)S(1)}, bf16[12,128,512]{2,1,0:T(8,128)(2,1)}, u32[]{:S(2)}, u32[]{:S(2)}) collective-permute-start(bf16[12,128,512]{2,1,0:T(8,128)(2,1)S(1)} %constant_dynamic-slice_fusion), channel_id=1, source_target_pairs={{0,1},{1,0},{2,3},{3,2},{4,5},{5,4},{6,7},{7,6},{8,9},{9,8},{10,11... | collective-permute-start | bytes 4718600 | tf_op jit(solution)/shard_map/cond/branch_1_fun/ppermute | solution.py:424
  7.0 6.1 %collective-permute-start.17 = (s32[8,136]{1,0:T(8,128)S(1)}, s32[8,136]{1,0:T(8,128)S(1)}, u32[]{:S(2)}, u32[]{:S(2)}) collective-permute-start(s32[8,136]{1,0:T(8,128)S(1)} %get-tuple-element.148), channel_id=1, source_target_pairs={{0,2},{1,3},{2,0},{3,1},{4,6},{5,7},{6,4},{7,5},{8,10},{9,11},{10,... | collective-permute-start | bytes 13064 | tf_op jit(solution)/shard_map/cond/branch_1_fun/ppermute | solution.py:421
  8.5 7.0 %collective-permute-start.18 = (s32[8,136]{1,0:T(8,128)S(1)}, s32[8,136]{1,0:T(8,128)S(1)}, u32[]{:S(2)}, u32[]{:S(2)}) collective-permute-start(s32[8,136]{1,0:T(8,128)S(1)} %get-tuple-element.148), channel_id=1, source_target_pairs={{0,4},{1,5},{2,6},{3,7},{4,0},{5,1},{6,2},{7,3},{8,12},{9,13},{10,... | collective-permute-start | bytes 13064 | tf_op jit(solution)/shard_map/cond/branch_1_fun/ppermute | solution.py:421
  11.4 25.1 %collective-permute-start.12 = (bf16[4,128,512]{2,1,0:T(8,128)(2,1)S(1)}, bf16[4,128,512]{2,1,0:T(8,128)(2,1)}, u32[]{:S(2)}, u32[]{:S(2)}) collective-permute-start(bf16[4,128,512]{2,1,0:T(8,128)(2,1)S(1)} %get-tuple-element.142), channel_id=1, source_target_pairs={{0,4},{1,5},{2,6},{3,7},{4,0},{5,1},{6,2},{7,3},{8,12},{9,13},{10,... | collective-permute-start | bytes 1572872 | tf_op jit(solution)/shard_map/cond/branch_1_fun/ppermute | solution.py:421
  13.0 23.5 %collective-permute-start.13 = (bf16[4,128,512]{2,1,0:T(8,128)(2,1)S(1)}, bf16[4,128,512]{2,1,0:T(8,128)(2,1)}, u32[]{:S(2)}, u32[]{:S(2)}) collective-permute-start(bf16[4,128,512]{2,1,0:T(8,128)(2,1)S(1)} %get-tuple-element.142), channel_id=1, source_target_pairs={{0,2},{1,3},{2,0},{3,1},{4,6},{5,7},{6,4},{7,5},{8,10},{9,11},{10,... | collective-permute-start | bytes 1572872 | tf_op jit(solution)/shard_map/cond/branch_1_fun/ppermute | solution.py:421
  41.5 15.3 %collective-permute-start.16 = (bf16[12,128,512]{2,1,0:T(8,128)(2,1)}, bf16[12,128,512]{2,1,0:T(8,128)(2,1)}, u32[]{:S(2)}, u32[]{:S(2)}) collective-permute-start(bf16[12,128,512]{2,1,0:T(8,128)(2,1)} %collective-permute-done.14), channel_id=1, source_target_pairs={{0,8},{8,0},{16,24},{24,16},{1,9},{9,1},{17,25},{25,17},{2,10},{10... | collective-permute-start | bytes 4718600 | tf_op jit(solution)/shard_map/cond/branch_1_fun/ppermute | solution.py:430
  42.0 14.8 %collective-permute-start.15 = (bf16[4,128,512]{2,1,0:T(8,128)(2,1)}, bf16[4,128,512]{2,1,0:T(8,128)(2,1)}, u32[]{:S(2)}, u32[]{:S(2)}) collective-permute-start(bf16[4,128,512]{2,1,0:T(8,128)(2,1)} %collective-permute-done.12), channel_id=1, source_target_pairs={{0,2},{1,3},{2,0},{3,1},{4,6},{5,7},{6,4},{7,5},{8,10},{9,11},{10,... | collective-permute-start | bytes 1572872 | tf_op jit(solution)/shard_map/cond/branch_1_fun/ppermute | solution.py:421
  56.8 28.0 %collective-permute-start = (bf16[4,128,512]{2,1,0:T(8,128)(2,1)S(1)}, bf16[4,128,512]{2,1,0:T(8,128)(2,1)}, u32[]{:S(2)}, u32[]{:S(2)}) collective-permute-start(bf16[4,128,512]{2,1,0:T(8,128)(2,1)S(1)} %get-tuple-element.151), channel_id=1, source_target_pairs={{0,4},{1,5},{2,6},{3,7},{4,0},{5,1},{6,2},{7,3},{8,12},{9,13},{10,... | collective-permute-start | bytes 1572872 | tf_op jit(solution)/shard_map/cond/branch_1_fun/ppermute | solution.py:421
  59.5 25.2 %collective-permute-start.1 = (bf16[4,128,512]{2,1,0:T(8,128)(2,1)S(1)}, bf16[4,128,512]{2,1,0:T(8,128)(2,1)}, u32[]{:S(2)}, u32[]{:S(2)}) collective-permute-start(bf16[4,128,512]{2,1,0:T(8,128)(2,1)S(1)} %get-tuple-element.151), channel_id=1, source_target_pairs={{0,2},{1,3},{2,0},{3,1},{4,6},{5,7},{6,4},{7,5},{8,10},{9,11},{10,... | collective-permute-start | bytes 1572872 | tf_op jit(solution)/shard_map/cond/branch_1_fun/ppermute | solution.py:421
  69.8 13.9 %collective-permute-start.2 = (f32[2,16,128]{2,1,0:T(8,128)S(1)}, f32[2,16,128]{2,1,0:T(8,128)S(1)}, u32[]{:S(2)}, u32[]{:S(2)}) collective-permute-start(f32[2,16,128]{2,1,0:T(8,128)S(1)} %get-tuple-element.166.refs_0_), channel_id=1, source_target_pairs={{0,2},{1,3},{2,0},{3,1},{4,6},{5,7},{6,4},{7,5},{8,10},{9,11},{10,... | collective-permute-start | bytes 49160 | tf_op jit(solution)/shard_map/cond/branch_1_fun/ppermute | solution.py:421
  69.9 13.8 %collective-permute-start.3 = (f32[2,16,128]{2,1,0:T(8,128)S(1)}, f32[2,16,128]{2,1,0:T(8,128)S(1)}, u32[]{:S(2)}, u32[]{:S(2)}) collective-permute-start(f32[2,16,128]{2,1,0:T(8,128)S(1)} %get-tuple-element.166.refs_0_), channel_id=1, source_target_pairs={{0,4},{1,5},{2,6},{3,7},{4,0},{5,1},{6,2},{7,3},{8,12},{9,13},{10,... | collective-permute-start | bytes 49160 | tf_op jit(solution)/shard_map/cond/branch_1_fun/ppermute | solution.py:421
  71.1 13.6 %collective-permute-start.4 = (f32[2,16,128]{2,1,0:T(8,128)S(1)}, f32[2,16,128]{2,1,0:T(8,128)S(1)}, u32[]{:S(2)}, u32[]{:S(2)}) collective-permute-start(f32[2,16,128]{2,1,0:T(8,128)S(1)} %get-tuple-element.166.refs_0_), channel_id=1, source_target_pairs={{0,6},{1,7},{2,4},{3,5},{4,2},{5,3},{6,0},{7,1},{8,14},{9,15},{10,... | collective-permute-start | bytes 49160 | tf_op jit(solution)/shard_map/cond/branch_1_fun/ppermute | solution.py:421
  84.8 12.8 %collective-permute-start.5 = (bf16[4,128,512]{2,1,0:T(8,128)(2,1)}, bf16[4,128,512]{2,1,0:T(8,128)(2,1)}, u32[]{:S(2)}, u32[]{:S(2)}) collective-permute-start(bf16[4,128,512]{2,1,0:T(8,128)(2,1)} %collective-permute-done), channel_id=1, source_target_pairs={{0,2},{1,3},{2,0},{3,1},{4,6},{5,7},{6,4},{7,5},{8,10},{9,11},{10,... | collective-permute-start | bytes 1572872 | tf_op jit(solution)/shard_map/cond/branch_1_fun/ppermute | solution.py:421
  98.5 18.6 %collective-permute-start.6 = (bf16[4,128,512]{2,1,0:T(8,128)(2,1)S(1)}, bf16[4,128,512]{2,1,0:T(8,128)(2,1)S(1)}, u32[]{:S(2)}, u32[]{:S(2)}) collective-permute-start(bf16[4,128,512]{2,1,0:T(8,128)(2,1)S(1)} %get-tuple-element.181), channel_id=1, source_target_pairs={{0,2},{1,3},{2,0},{3,1},{4,6},{5,7},{6,4},{7,5},{8,10},{9,11},{10,... | collective-permute-start | bytes 1572872 | tf_op jit(solution)/shard_map/cond/branch_1_fun/ppermute | solution.py:421
  111.3 21.5 %collective-permute-start.10 = (bf16[4,128,512]{2,1,0:T(8,128)(2,1)}, bf16[4,128,512]{2,1,0:T(8,128)(2,1)S(1)}, u32[]{:S(2)}, u32[]{:S(2)}) collective-permute-start(bf16[4,128,512]{2,1,0:T(8,128)(2,1)} %get-tuple-element.201), channel_id=1, source_target_pairs={{0,2},{1,3},{2,0},{3,1},{4,6},{5,7},{6,4},{7,5},{8,10},{9,11},{10,... | collective-permute-start | bytes 1572872 | tf_op jit(solution)/shard_map/cond/branch_1_fun/ppermute | solution.py:421
  117.3 22.9 %collective-permute-start.11 = (bf16[4,128,512]{2,1,0:T(8,128)(2,1)S(1)}, bf16[4,128,512]{2,1,0:T(8,128)(2,1)S(1)}, u32[]{:S(2)}, u32[]{:S(2)}) collective-permute-start(bf16[4,128,512]{2,1,0:T(8,128)(2,1)S(1)} %add_convert_fusion), channel_id=1, source_target_pairs={{0,4},{1,5},{2,6},{3,7},{4,0},{5,1},{6,2},{7,3},{8,12},{9,13},{10,... | collective-permute-start | bytes 1572872 | tf_op jit(solution)/shard_map/cond/branch_1_fun/ppermute | solution.py:421
  140.4 5.9 %collective-permute-start.22 = (bf16[2,2,24,128,128]{4,3,2,1,0:T(8,128)(2,1)}, bf16[2,2,24,128,128]{4,3,2,1,0:T(8,128)(2,1)S(1)}, u32[]{:S(2)}, u32[]{:S(2)}) collective-permute-start(bf16[2,2,24,128,128]{4,3,2,1,0:T(8,128)(2,1)} %get-tuple-element.274), channel_id=1, source_target_pairs={{0,8},{8,0},{16,24},{24,16},{1,9},{9,1},{17,25},{25,17},{2,10},{10... | collective-permute-start | bytes 9437192 | tf_op jit(solution)/shard_map/ppermute | solution.py:430
  140.5 15.0 %collective-permute-start.21 = (bf16[4,128,512]{2,1,0:T(8,128)(2,1)}, bf16[4,128,512]{2,1,0:T(8,128)(2,1)S(1)}, u32[]{:S(2)}, u32[]{:S(2)}) collective-permute-start(bf16[4,128,512]{2,1,0:T(8,128)(2,1)} %get-tuple-element.272), channel_id=1, source_target_pairs={{0,2},{1,3},{2,0},{3,1},{4,6},{5,7},{6,4},{7,5},{8,10},{9,11},{10,... | collective-permute-start | bytes 1572872 | tf_op jit(solution)/shard_map/ppermute | solution.py:421
  140.6 32.6 %collective-permute-start.20 = (bf16[4,128,512]{2,1,0:T(8,128)(2,1)}, bf16[4,128,512]{2,1,0:T(8,128)(2,1)S(1)}, u32[]{:S(2)}, u32[]{:S(2)}) collective-permute-start(bf16[4,128,512]{2,1,0:T(8,128)(2,1)} %get-tuple-element.271), channel_id=1, source_target_pairs={{0,2},{1,3},{2,0},{3,1},{4,6},{5,7},{6,4},{7,5},{8,10},{9,11},{10,... | collective-permute-start | bytes 1572872 | tf_op jit(solution)/shard_map/ppermute | solution.py:421
  155.7 25.3 %collective-permute-start.23 = (bf16[4,128,512]{2,1,0:T(8,128)(2,1)S(1)}, bf16[4,128,512]{2,1,0:T(8,128)(2,1)S(1)}, u32[]{:S(2)}, u32[]{:S(2)}) collective-permute-start(bf16[4,128,512]{2,1,0:T(8,128)(2,1)S(1)} %add_convert_fusion.3), channel_id=1, source_target_pairs={{0,4},{1,5},{2,6},{3,7},{4,0},{5,1},{6,2},{7,3},{8,12},{9,13},{10,... | collective-permute-start | bytes 1572872 | tf_op jit(solution)/shard_map/ppermute | solution.py:421
  155.8 25.7 %collective-permute-start.25 = (bf16[2,12,128,128]{3,2,1,0:T(8,128)(2,1)S(1)}, bf16[2,12,128,128]{3,2,1,0:T(8,128)(2,1)S(1)}, u32[]{:S(2)}, u32[]{:S(2)}) collective-permute-start(bf16[2,12,128,128]{3,2,1,0:T(8,128)(2,1)S(1)} %fusion.23), channel_id=1, source_target_pairs={{0,16},{8,24},{16,0},{24,8},{1,17},{9,25},{17,1},{25,9},{2,18},{10... | collective-permute-start | bytes 2359304 | tf_op jit(solution)/shard_map/ppermute | solution.py:427
  157.8 23.7 %collective-permute-start.24 = (bf16[2,12,128,128]{3,2,1,0:T(8,128)(2,1)S(1)}, bf16[2,12,128,128]{3,2,1,0:T(8,128)(2,1)S(1)}, u32[]{:S(2)}, u32[]{:S(2)}) collective-permute-start(bf16[2,12,128,128]{3,2,1,0:T(8,128)(2,1)S(1)} %fusion.22), channel_id=1, source_target_pairs={{0,1},{1,0},{2,3},{3,2},{4,5},{5,4},{6,7},{7,6},{8,9},{9,8},{10,11... | collective-permute-start | bytes 2359304 | tf_op jit(solution)/shard_map/ppermute | solution.py:424
  182.0 9.6 %collective-permute-start.26 = (bf16[12,128,128]{2,1,0:T(8,128)(2,1)S(1)}, bf16[12,128,128]{2,1,0:T(8,128)(2,1)S(1)}, u32[]{:S(2)}, u32[]{:S(2)}) collective-permute-start(bf16[12,128,128]{2,1,0:T(8,128)(2,1)S(1)} %get-tuple-element.304), channel_id=1, source_target_pairs={{0,16},{8,24},{16,0},{24,8},{1,17},{9,25},{17,1},{25,9},{2,18},{10... | collective-permute-start | bytes 1179656 | tf_op jit(solution)/shard_map/ppermute | solution.py:427
  183.9 9.1 %collective-permute-start.27 = (bf16[12,128,128]{2,1,0:T(8,128)(2,1)S(1)}, bf16[12,128,128]{2,1,0:T(8,128)(2,1)S(1)}, u32[]{:S(2)}, u32[]{:S(2)}) collective-permute-start(bf16[12,128,128]{2,1,0:T(8,128)(2,1)S(1)} %get-tuple-element.303), channel_id=1, source_target_pairs={{0,1},{1,0},{2,3},{3,2},{4,5},{5,4},{6,7},{7,6},{8,9},{9,8},{10,11... | collective-permute-start | bytes 1179656 | tf_op jit(solution)/shard_map/ppermute | solution.py:424
  (17 other events, 217.3 us)
where the time goes:
time: 195 us
  waiting for transfers between devices  105 us (54%)
  Pallas kernels  37 us (19%)
  starting transfers between devices  36.7 us (19%)
  other arithmetic  10.2 us (5%)
  local copies, waits for them, and re-layouts  4.8 us (2%)
    ppermute x21, waiting for transfers between devices, over_z(): return lax.ppermute(value, 'cls', pairs)  90.3 us
    ppermute x21, starting transfers between devices, over_z(): return lax.ppermute(value, 'cls', pairs)  28.6 us
    pallas_call x2, Pallas kernels, score(): pl.pallas_call(functools.partial(score_kernel, len(rows), len(tables), bl...  15.4 us
    pallas_call x1, Pallas kernels, last_grads(): pl.pallas_call(functools.partial(last_kernel, sizes, len(shapes), len(tab...  13 us
    pallas_call x1, Pallas kernels, grads(): pl.pallas_call(functools.partial(grad_kernel, len(shapes), len(tables), l...  8.65 us
    ppermute x3, waiting for transfers between devices, over_x(): lax.ppermute(value, 'cls', [(c, c ^ 1) for c in range(self.nx * self.nz)])  6.42 us
    ppermute x2, waiting for transfers between devices, over_y(): return lax.ppermute(value, 'dp', [(d, d ^ 2) for d in range(self.dp)])  5.09 us
    ppermute x3, starting transfers between devices, over_x(): lax.ppermute(value, 'cls', [(c, c ^ 1) for c in range(self.nx * self.nz)])  4.08 us
  transfers between devices with their start and end apart: 28, of which 17 were waited for; matrix products, arithmetic and copies ran while one was open for 4% of the time, Pallas kernels for 19%

commit v1 on v0

--- a/solution.py
+++ b/solution.py
@@ -495,21 +495,23 @@
         y_sent = add(kept[:, 1, half:], got[:, 1, half:])
         passed, _, _ = lax.optimization_barrier((passed, x_sent, y_sent))
         far = self.over_z(add(passed, parts[2]), 2)
-        total = sum(part.astype(jnp.float32) for part in (parts[0], near, far))
-        return total, self.sum_shares(kept, got, x_sent, y_sent)
+        near, far, shares = self.sum_shares(near, far, kept, got, x_sent, y_sent)
+        return sum(part.astype(jnp.float32) for part in (parts[0], near, far)), shares
 
     def share_shapes(self, shard_tiles):
         return [(self.nx, self.dp // 2, shard_tiles, TILE, D // self.dp)] * 2
 
-    def sum_shares(self, kept, got, x_sent, y_sent):
+    def sum_shares(self, near, far, kept, got, x_sent, y_sent):
         half = kept.shape[2] // 2
         x_got, y_got = lax.optimization_barrier((self.over_x(x_sent), self.over_y(y_sent)))
         x_kept = [add(add(kept[0, y, :half], got[0, y, :half]), x_got[y]) for y in range(2)]
         y_kept = [add(add(kept[x, 0, half:], got[x, 0, half:]), y_got[x]) for x in range(2)]
-        low, high = lax.optimization_barrier((self.over_y(x_kept[1]), self.over_x(y_kept[1])))
+        near, far, low, high = lax.optimization_barrier(
+            (near, far, self.over_y(x_kept[1]), self.over_x(y_kept[1]))
+        )
         low = x_kept[0].astype(jnp.float32) + low.astype(jnp.float32)
         high = y_kept[0].astype(jnp.float32) + high.astype(jnp.float32)
-        return jnp.concatenate([low, high], axis=0)
+        return near, far, jnp.concatenate([low, high], axis=0)
 
 
 class Groups:

time: 195 us -> 185 us (0.949)
  waiting for transfers between devices: 105 us -> 96.1 us
    ppermute x21, waiting for transfers between devices: 90.3 us -> 73.3 us  [over_z(): return lax.ppermute(value, 'cls', pairs)]
    ppermute x2, waiting for transfers between devices: 5.09 us -> 10.5 us  [over_y(): return lax.ppermute(value, 'dp', [(d, d ^ 2) for d in range(self.dp)])]
    ppermute x2, waiting for transfers between devices: 2.89 us -> 5.78 us  [over_core(): return lax.ppermute(value, 'dp', [(d, d ^ 1) for d in range(self.dp)])]
    ppermute x21, starting transfers between devices: 28.6 us -> 26.1 us  [over_z(): return lax.ppermute(value, 'cls', pairs)]
  transfers between devices with their start and end apart: 28 -> 28, of which waited for: 17 -> 17; matrix products, arithmetic and copies ran while one was open for 4% -> 4% of each run, Pallas kernels for 19% -> 20%
where the time goes in v1:
time: 185 us
  waiting for transfers between devices  96.1 us (52%)
  Pallas kernels  37.9 us (20%)
  starting transfers between devices  34.8 us (19%)
  other arithmetic  10.3 us (6%)
  local copies, waits for them, and re-layouts  4.79 us (3%)
    ppermute x21, waiting for transfers between devices, over_z(): return lax.ppermute(value, 'cls', pairs)  73.3 us
    ppermute x21, starting transfers between devices, over_z(): return lax.ppermute(value, 'cls', pairs)  26.1 us
    pallas_call x2, Pallas kernels, score(): pl.pallas_call(functools.partial(score_kernel, len(rows), len(tables), bl...  15.3 us
    pallas_call x1, Pallas kernels, last_grads(): pl.pallas_call(functools.partial(last_kernel, sizes, len(shapes), len(tab...  13.8 us
    ppermute x2, waiting for transfers between devices, over_y(): return lax.ppermute(value, 'dp', [(d, d ^ 2) for d in range(self.dp)])  10.5 us
    pallas_call x1, Pallas kernels, grads(): pl.pallas_call(functools.partial(grad_kernel, len(shapes), len(tables), l...  8.87 us
    ppermute x3, waiting for transfers between devices, over_x(): lax.ppermute(value, 'cls', [(c, c ^ 1) for c in range(self.nx * self.nz)])  6.51 us
    ppermute x3, starting transfers between devices, over_x(): lax.ppermute(value, 'cls', [(c, c ^ 1) for c in range(self.nx * self.nz)])  5.91 us
  transfers between devices with their start and end apart: 28, of which 17 were waited for; matrix products, arithmetic and copies ran while one was open for 4% of the time, Pallas kernels for 20%

profile of v1, /device:TPU:0, one launch (start us, length us, event | category | flops | bytes accessed | tf_op | source)
XLA Modules:
  0.0 185.1 jit_solution(15469314968696490083)
XLA Ops:
  2.4 54.4 %conditional.3 = (bf16[4,128,512]{2,1,0:T(8,128)(2,1)}, bf16[4,128,512]{2,1,0:T(8,128)(2,1)}, bf16[4,128,512]{2,1,0:T(8,128)(2,1)}, bf16[12,128,512]{2,1,0:T(8,1...) conditional(s32[]{:T(128)} %bitcast.8, () %tuple.75, ...), branch_computations={%region_0.1_spmd, %region_1.8_spmd} | conditional | flops 232492 | bytes 22230328 | solution.py:487
  3.9 3.0 %collective-permute-start.14 = (bf16[12,128,512]{2,1,0:T(8,128)(2,1)S(1)}, bf16[12,128,512]{2,1,0:T(8,128)(2,1)}, u32[]{:S(2)}, u32[]{:S(2)}) collective-permute-start(bf16[12,128,512]{2,1,0:T(8,128)(2,1)S(1)} %constant_dynamic-slice_fusion), channel_id=1, source_target_pairs={{0,1},{1,0},{2,3},{3,2},{4,5},{5,4},{6,7},{7,6},{8,9},{9,8},{10,11... | collective-permute-start | bytes 4718600 | tf_op jit(solution)/shard_map/cond/branch_1_fun/ppermute | solution.py:424
  8.5 2.6 %collective-permute-start.18 = (s32[8,136]{1,0:T(8,128)S(1)}, s32[8,136]{1,0:T(8,128)S(1)}, u32[]{:S(2)}, u32[]{:S(2)}) collective-permute-start(s32[8,136]{1,0:T(8,128)S(1)} %get-tuple-element.148), channel_id=1, source_target_pairs={{0,4},{1,5},{2,6},{3,7},{4,0},{5,1},{6,2},{7,3},{8,12},{9,13},{10,... | collective-permute-start | bytes 13064 | tf_op jit(solution)/shard_map/cond/branch_1_fun/ppermute | solution.py:421
  13.0 2.5 %collective-permute-start.13 = (bf16[4,128,512]{2,1,0:T(8,128)(2,1)S(1)}, bf16[4,128,512]{2,1,0:T(8,128)(2,1)}, u32[]{:S(2)}, u32[]{:S(2)}) collective-permute-start(bf16[4,128,512]{2,1,0:T(8,128)(2,1)S(1)} %get-tuple-element.142), channel_id=1, source_target_pairs={{0,2},{1,3},{2,0},{3,1},{4,6},{5,7},{6,4},{7,5},{8,10},{9,11},{10,... | collective-permute-start | bytes 1572872 | tf_op jit(solution)/shard_map/cond/branch_1_fun/ppermute | solution.py:421
  19.2 17.3 %collective-permute-done.12 = bf16[4,128,512]{2,1,0:T(8,128)(2,1)} collective-permute-done((bf16[4,128,512]{2,1,0:T(8,128)(2,1)S(1)}, bf16[4,128,512]{2,1,0:T(8,128)(2,1)}, u32[]{:S(2)}, u32[]{:S(2)}) %collective-permute-start.12) | collective-permute-done | bytes 524320 | tf_op jit(solution)/shard_map/cond/branch_1_fun/ppermute | solution.py:421
  36.5 5.0 %collective-permute-done.14 = bf16[12,128,512]{2,1,0:T(8,128)(2,1)} collective-permute-done((bf16[12,128,512]{2,1,0:T(8,128)(2,1)S(1)}, bf16[12,128,512]{2,1,0:T(8,128)(2,1)}, u32[]{:S(2)}, u32[]{:S(2)}) %collective-permute-start.14) | collective-permute-done | bytes 1572896 | tf_op jit(solution)/shard_map/cond/branch_1_fun/ppermute | solution.py:424
  44.6 12.2 %collective-permute-done.15 = bf16[4,128,512]{2,1,0:T(8,128)(2,1)} collective-permute-done((bf16[4,128,512]{2,1,0:T(8,128)(2,1)}, bf16[4,128,512]{2,1,0:T(8,128)(2,1)}, u32[]{:S(2)}, u32[]{:S(2)}) %collective-permute-start.15) | collective-permute-done | bytes 524320 | tf_op jit(solution)/shard_map/cond/branch_1_fun/ppermute | solution.py:421
  56.8 40.7 %conditional.4 = (bf16[4,128,512]{2,1,0:T(8,128)(2,1)}, bf16[4,128,512]{2,1,0:T(8,128)(2,1)}, bf16[4,128,512]{2,1,0:T(8,128)(2,1)}, bf16[16,128,512]{2,1,0:T(8,1...) conditional(s32[]{:T(128)} %bitcast.8, () %tuple.74, ...), branch_computations={%region_8.9_spmd, %region_9.10_spmd} | conditional | flops 2359296 | bytes 22745436 | solution.py:487
  56.8 2.8 %collective-permute-start = (bf16[4,128,512]{2,1,0:T(8,128)(2,1)S(1)}, bf16[4,128,512]{2,1,0:T(8,128)(2,1)}, u32[]{:S(2)}, u32[]{:S(2)}) collective-permute-start(bf16[4,128,512]{2,1,0:T(8,128)(2,1)S(1)} %get-tuple-element.151), channel_id=1, source_target_pairs={{0,4},{1,5},{2,6},{3,7},{4,0},{5,1},{6,2},{7,3},{8,12},{9,13},{10,... | collective-permute-start | bytes 1572872 | tf_op jit(solution)/shard_map/cond/branch_1_fun/ppermute | solution.py:421
  61.1 8.0 %branch_1_fun.4 = (f32[2,16,128]{2,1,0:T(8,128)S(1)}, bf16[16,128,512]{2,1,0:T(8,128)(2,1)}) custom-call(s32[64]{0:T(128)S(1)} %get-tuple-element.152.codes_ref, s32[3]{0:T(128)S(1)} %get-tuple-element.153.meta_ref, s32[16,128]{1,0:T(8,128)S(1)} %get-tuple-element.154.hit_ref, bf16[4,128,512]{2,1,0:T(8,128)(2,1)S(1)} %get-tuple-element.155.refs_0_, ...), custom_call_target="tpu_custom_call" | custom-call | flops 1048576 | bytes 1048576 | tf_op jit(solution)/shard_map/cond/branch_1_fun/pallas_call | solution.py:315
  70.5 3.0 %collective-permute-start.4 = (f32[2,16,128]{2,1,0:T(8,128)S(1)}, f32[2,16,128]{2,1,0:T(8,128)S(1)}, u32[]{:S(2)}, u32[]{:S(2)}) collective-permute-start(f32[2,16,128]{2,1,0:T(8,128)S(1)} %get-tuple-element.166.refs_0_), channel_id=1, source_target_pairs={{0,6},{1,7},{2,4},{3,5},{4,2},{5,3},{6,0},{7,1},{8,14},{9,15},{10,... | collective-permute-start | bytes 49160 | tf_op jit(solution)/shard_map/cond/branch_1_fun/ppermute | solution.py:421
  73.5 10.2 %collective-permute-done.2.refs_1_ = f32[2,16,128]{2,1,0:T(8,128)S(1)} collective-permute-done((f32[2,16,128]{2,1,0:T(8,128)S(1)}, f32[2,16,128]{2,1,0:T(8,128)S(1)}, u32[]{:S(2)}, u32[]{:S(2)}) %collective-permute-start.2) | collective-permute-done | bytes 16416 | tf_op jit(solution)/shard_map/cond/branch_1_fun/ppermute | solution.py:421
  85.2 8.9 %branch_1_fun.5 = (bf16[4,128,512]{2,1,0:T(8,128)(2,1)S(1)}, bf16[4,128,512]{2,1,0:T(8,128)(2,1)}, bf16[4,128,512]{2,1,0:T(8,128)(2,1)S(1)}, bf16[4,128,512]{2,1...) custom-call(s32[64]{0:T(128)S(1)} %get-tuple-element.152.codes_ref, ...), custom_call_target="tpu_custom_call" | custom-call | flops 1048576 | bytes 1048576 | tf_op jit(solution)/shard_map/cond/branch_1_fun/pallas_call | solution.py:339
  94.2 3.3 %collective-permute-done.5 = bf16[4,128,512]{2,1,0:T(8,128)(2,1)} collective-permute-done((bf16[4,128,512]{2,1,0:T(8,128)(2,1)}, bf16[4,128,512]{2,1,0:T(8,128)(2,1)}, u32[]{:S(2)}, u32[]{:S(2)}) %collective-permute-start.5) | collective-permute-done | bytes 524320 | tf_op jit(solution)/shard_map/cond/branch_1_fun/ppermute | solution.py:421
  98.5 41.8 %conditional.5 = (bf16[4,128,512]{2,1,0:T(8,128)(2,1)}, bf16[4,128,512]{2,1,0:T(8,128)(2,1)}, bf16[2,2,24,128,128]{4,3,2,1,0:T(8,128)(2,1)S(1)}, bf16[2,2,24,128...) conditional(s32[]{:T(128)} %bitcast.8, () %tuple.78, ...), branch_computations={%region_10.11_spmd, %region_11.12_spmd} | conditional | flops 5242880 | bytes 38474096 | solution.py:487
  99.5 7.4 %branch_1_fun.6 = (f32[2,16,128]{2,1,0:T(8,128)S(1)}, bf16[16,128,512]{2,1,0:T(8,128)(2,1)S(1)}) custom-call(s32[64]{0:T(128)S(1)} %get-tuple-element.177.codes_ref.refs_1_, s32[3]{0:T(128)S(1)} %get-tuple-element.179.meta_ref.refs_3_, s32[16,128]{1,0:T(8,128)S(1)} %get-tuple-element.180.hit_ref.refs_4_, ...), custom_call_target="tpu_custom_call" | custom-call | flops 1048576 | bytes 1048576 | tf_op jit(solution)/shard_map/cond/branch_1_fun/pallas_call | solution.py:315
  107.9 2.2 %collective-permute-start.8 = (f32[2,16,128]{2,1,0:T(8,128)S(1)}, f32[2,16,128]{2,1,0:T(8,128)S(1)}, u32[]{:S(2)}, u32[]{:S(2)}) collective-permute-start(f32[2,16,128]{2,1,0:T(8,128)S(1)} %get-tuple-element.190.refs_5_), channel_id=1, source_target_pairs={{0,4},{1,5},{2,6},{3,7},{4,0},{5,1},{6,2},{7,3},{8,12},{9,13},{10,... | collective-permute-start | bytes 49160 | tf_op jit(solution)/shard_map/cond/branch_1_fun/ppermute | solution.py:421
  112.7 3.8 %collective-permute-done.9.refs_8_ = f32[2,16,128]{2,1,0:T(8,128)S(1)} collective-permute-done((f32[2,16,128]{2,1,0:T(8,128)S(1)}, f32[2,16,128]{2,1,0:T(8,128)S(1)}, u32[]{:S(2)}, u32[]{:S(2)}) %collective-permute-start.9) | collective-permute-done | bytes 16416 | tf_op jit(solution)/shard_map/cond/branch_1_fun/ppermute | solution.py:421
  116.8 13.8 %branch_1_fun.7 = (bf16[4,128,512]{2,1,0:T(8,128)(2,1)S(1)}, bf16[4,128,512]{2,1,0:T(8,128)(2,1)}, bf16[4,128,512]{2,1,0:T(8,128)(2,1)S(1)}, bf16[4,128,512]{2,1...) custom-call(s32[64]{0:T(128)S(1)} %get-tuple-element.176.refs_0_, ...), custom_call_target="tpu_custom_call" | custom-call | flops 2097152 | bytes 2097152 | tf_op jit(solution)/shard_map/cond/branch_1_fun/pallas_call | solution.py:374
  132.9 7.1 %collective-permute-done.11 = bf16[4,128,512]{2,1,0:T(8,128)(2,1)S(1)} collective-permute-done((bf16[4,128,512]{2,1,0:T(8,128)(2,1)S(1)}, bf16[4,128,512]{2,1,0:T(8,128)(2,1)S(1)}, u32[]{:S(2)}, u32[]{:S(2)}) %collective-permute-start.11) | collective-permute-done | bytes 524320 | tf_op jit(solution)/shard_map/cond/branch_1_fun/ppermute | solution.py:421
  140.5 5.8 %collective-permute-done.22 = bf16[2,2,24,128,128]{4,3,2,1,0:T(8,128)(2,1)S(1)} collective-permute-done((bf16[2,2,24,128,128]{4,3,2,1,0:T(8,128)(2,1)}, bf16[2,2,24,128,128]{4,3,2,1,0:T(8,128)(2,1)S(1)}, u32[]{:S(2)}, u32[]{:S(2)}) %collective-permute-start.22) | collective-permute-done | bytes 3145760 | tf_op jit(solution)/shard_map/ppermute | solution.py:430
  149.8 5.6 %collective-permute-done.21 = bf16[4,128,512]{2,1,0:T(8,128)(2,1)S(1)} collective-permute-done((bf16[4,128,512]{2,1,0:T(8,128)(2,1)}, bf16[4,128,512]{2,1,0:T(8,128)(2,1)S(1)}, u32[]{:S(2)}, u32[]{:S(2)}) %collective-permute-start.21) | collective-permute-done | bytes 524320 | tf_op jit(solution)/shard_map/ppermute | solution.py:421
  155.7 10.5 %collective-permute-done.25 = bf16[2,12,128,128]{3,2,1,0:T(8,128)(2,1)S(1)} collective-permute-done((bf16[2,12,128,128]{3,2,1,0:T(8,128)(2,1)S(1)}, bf16[2,12,128,128]{3,2,1,0:T(8,128)(2,1)S(1)}, u32[]{:S(2)}, u32[]{:S(2)}) %collective-permute-start.25) | collective-permute-done | bytes 786464 | tf_op jit(solution)/shard_map/ppermute | solution.py:427
  173.1 7.8 %collective-permute-done.23 = bf16[4,128,512]{2,1,0:T(8,128)(2,1)S(1)} collective-permute-done((bf16[4,128,512]{2,1,0:T(8,128)(2,1)S(1)}, bf16[4,128,512]{2,1,0:T(8,128)(2,1)S(1)}, u32[]{:S(2)}, u32[]{:S(2)}) %collective-permute-start.23) | collective-permute-done | bytes 524320 | tf_op jit(solution)/shard_map/ppermute | solution.py:421
  (114 shorter events, 41.4 us)
Async XLA Ops:
  3.9 37.5 %collective-permute-start.14 = (bf16[12,128,512]{2,1,0:T(8,128)(2,1)S(1)}, bf16[12,128,512]{2,1,0:T(8,128)(2,1)}, u32[]{:S(2)}, u32[]{:S(2)}) collective-permute-start(bf16[12,128,512]{2,1,0:T(8,128)(2,1)S(1)} %constant_dynamic-slice_fusion), channel_id=1, source_target_pairs={{0,1},{1,0},{2,3},{3,2},{4,5},{5,4},{6,7},{7,6},{8,9},{9,8},{10,11... | collective-permute-start | bytes 4718600 | tf_op jit(solution)/shard_map/cond/branch_1_fun/ppermute | solution.py:424
  7.0 6.1 %collective-permute-start.17 = (s32[8,136]{1,0:T(8,128)S(1)}, s32[8,136]{1,0:T(8,128)S(1)}, u32[]{:S(2)}, u32[]{:S(2)}) collective-permute-start(s32[8,136]{1,0:T(8,128)S(1)} %get-tuple-element.148), channel_id=1, source_target_pairs={{0,2},{1,3},{2,0},{3,1},{4,6},{5,7},{6,4},{7,5},{8,10},{9,11},{10,... | collective-permute-start | bytes 13064 | tf_op jit(solution)/shard_map/cond/branch_1_fun/ppermute | solution.py:421
  8.5 7.0 %collective-permute-start.18 = (s32[8,136]{1,0:T(8,128)S(1)}, s32[8,136]{1,0:T(8,128)S(1)}, u32[]{:S(2)}, u32[]{:S(2)}) collective-permute-start(s32[8,136]{1,0:T(8,128)S(1)} %get-tuple-element.148), channel_id=1, source_target_pairs={{0,4},{1,5},{2,6},{3,7},{4,0},{5,1},{6,2},{7,3},{8,12},{9,13},{10,... | collective-permute-start | bytes 13064 | tf_op jit(solution)/shard_map/cond/branch_1_fun/ppermute | solution.py:421
  11.3 25.1 %collective-permute-start.12 = (bf16[4,128,512]{2,1,0:T(8,128)(2,1)S(1)}, bf16[4,128,512]{2,1,0:T(8,128)(2,1)}, u32[]{:S(2)}, u32[]{:S(2)}) collective-permute-start(bf16[4,128,512]{2,1,0:T(8,128)(2,1)S(1)} %get-tuple-element.142), channel_id=1, source_target_pairs={{0,4},{1,5},{2,6},{3,7},{4,0},{5,1},{6,2},{7,3},{8,12},{9,13},{10,... | collective-permute-start | bytes 1572872 | tf_op jit(solution)/shard_map/cond/branch_1_fun/ppermute | solution.py:421
  13.0 23.5 %collective-permute-start.13 = (bf16[4,128,512]{2,1,0:T(8,128)(2,1)S(1)}, bf16[4,128,512]{2,1,0:T(8,128)(2,1)}, u32[]{:S(2)}, u32[]{:S(2)}) collective-permute-start(bf16[4,128,512]{2,1,0:T(8,128)(2,1)S(1)} %get-tuple-element.142), channel_id=1, source_target_pairs={{0,2},{1,3},{2,0},{3,1},{4,6},{5,7},{6,4},{7,5},{8,10},{9,11},{10,... | collective-permute-start | bytes 1572872 | tf_op jit(solution)/shard_map/cond/branch_1_fun/ppermute | solution.py:421
  41.5 15.3 %collective-permute-start.16 = (bf16[12,128,512]{2,1,0:T(8,128)(2,1)}, bf16[12,128,512]{2,1,0:T(8,128)(2,1)}, u32[]{:S(2)}, u32[]{:S(2)}) collective-permute-start(bf16[12,128,512]{2,1,0:T(8,128)(2,1)} %collective-permute-done.14), channel_id=1, source_target_pairs={{0,8},{8,0},{16,24},{24,16},{1,9},{9,1},{17,25},{25,17},{2,10},{10... | collective-permute-start | bytes 4718600 | tf_op jit(solution)/shard_map/cond/branch_1_fun/ppermute | solution.py:430
  42.0 14.8 %collective-permute-start.15 = (bf16[4,128,512]{2,1,0:T(8,128)(2,1)}, bf16[4,128,512]{2,1,0:T(8,128)(2,1)}, u32[]{:S(2)}, u32[]{:S(2)}) collective-permute-start(bf16[4,128,512]{2,1,0:T(8,128)(2,1)} %collective-permute-done.12), channel_id=1, source_target_pairs={{0,2},{1,3},{2,0},{3,1},{4,6},{5,7},{6,4},{7,5},{8,10},{9,11},{10,... | collective-permute-start | bytes 1572872 | tf_op jit(solution)/shard_map/cond/branch_1_fun/ppermute | solution.py:421
  56.8 28.0 %collective-permute-start = (bf16[4,128,512]{2,1,0:T(8,128)(2,1)S(1)}, bf16[4,128,512]{2,1,0:T(8,128)(2,1)}, u32[]{:S(2)}, u32[]{:S(2)}) collective-permute-start(bf16[4,128,512]{2,1,0:T(8,128)(2,1)S(1)} %get-tuple-element.151), channel_id=1, source_target_pairs={{0,4},{1,5},{2,6},{3,7},{4,0},{5,1},{6,2},{7,3},{8,12},{9,13},{10,... | collective-permute-start | bytes 1572872 | tf_op jit(solution)/shard_map/cond/branch_1_fun/ppermute | solution.py:421
  59.5 25.2 %collective-permute-start.1 = (bf16[4,128,512]{2,1,0:T(8,128)(2,1)S(1)}, bf16[4,128,512]{2,1,0:T(8,128)(2,1)}, u32[]{:S(2)}, u32[]{:S(2)}) collective-permute-start(bf16[4,128,512]{2,1,0:T(8,128)(2,1)S(1)} %get-tuple-element.151), channel_id=1, source_target_pairs={{0,2},{1,3},{2,0},{3,1},{4,6},{5,7},{6,4},{7,5},{8,10},{9,11},{10,... | collective-permute-start | bytes 1572872 | tf_op jit(solution)/shard_map/cond/branch_1_fun/ppermute | solution.py:421
  69.1 14.7 %collective-permute-start.2 = (f32[2,16,128]{2,1,0:T(8,128)S(1)}, f32[2,16,128]{2,1,0:T(8,128)S(1)}, u32[]{:S(2)}, u32[]{:S(2)}) collective-permute-start(f32[2,16,128]{2,1,0:T(8,128)S(1)} %get-tuple-element.166.refs_0_), channel_id=1, source_target_pairs={{0,2},{1,3},{2,0},{3,1},{4,6},{5,7},{6,4},{7,5},{8,10},{9,11},{10,... | collective-permute-start | bytes 49160 | tf_op jit(solution)/shard_map/cond/branch_1_fun/ppermute | solution.py:421
  69.2 14.6 %collective-permute-start.3 = (f32[2,16,128]{2,1,0:T(8,128)S(1)}, f32[2,16,128]{2,1,0:T(8,128)S(1)}, u32[]{:S(2)}, u32[]{:S(2)}) collective-permute-start(f32[2,16,128]{2,1,0:T(8,128)S(1)} %get-tuple-element.166.refs_0_), channel_id=1, source_target_pairs={{0,4},{1,5},{2,6},{3,7},{4,0},{5,1},{6,2},{7,3},{8,12},{9,13},{10,... | collective-permute-start | bytes 49160 | tf_op jit(solution)/shard_map/cond/branch_1_fun/ppermute | solution.py:421
  70.5 14.2 %collective-permute-start.4 = (f32[2,16,128]{2,1,0:T(8,128)S(1)}, f32[2,16,128]{2,1,0:T(8,128)S(1)}, u32[]{:S(2)}, u32[]{:S(2)}) collective-permute-start(f32[2,16,128]{2,1,0:T(8,128)S(1)} %get-tuple-element.166.refs_0_), channel_id=1, source_target_pairs={{0,6},{1,7},{2,4},{3,5},{4,2},{5,3},{6,0},{7,1},{8,14},{9,15},{10,... | collective-permute-start | bytes 49160 | tf_op jit(solution)/shard_map/cond/branch_1_fun/ppermute | solution.py:421
  84.7 12.8 %collective-permute-start.5 = (bf16[4,128,512]{2,1,0:T(8,128)(2,1)}, bf16[4,128,512]{2,1,0:T(8,128)(2,1)}, u32[]{:S(2)}, u32[]{:S(2)}) collective-permute-start(bf16[4,128,512]{2,1,0:T(8,128)(2,1)} %collective-permute-done), channel_id=1, source_target_pairs={{0,2},{1,3},{2,0},{3,1},{4,6},{5,7},{6,4},{7,5},{8,10},{9,11},{10,... | collective-permute-start | bytes 1572872 | tf_op jit(solution)/shard_map/cond/branch_1_fun/ppermute | solution.py:421
  98.5 18.1 %collective-permute-start.6 = (bf16[4,128,512]{2,1,0:T(8,128)(2,1)S(1)}, bf16[4,128,512]{2,1,0:T(8,128)(2,1)S(1)}, u32[]{:S(2)}, u32[]{:S(2)}) collective-permute-start(bf16[4,128,512]{2,1,0:T(8,128)(2,1)S(1)} %get-tuple-element.181), channel_id=1, source_target_pairs={{0,2},{1,3},{2,0},{3,1},{4,6},{5,7},{6,4},{7,5},{8,10},{9,11},{10,... | collective-permute-start | bytes 1572872 | tf_op jit(solution)/shard_map/cond/branch_1_fun/ppermute | solution.py:421
  110.1 6.4 %collective-permute-start.9 = (f32[2,16,128]{2,1,0:T(8,128)S(1)}, f32[2,16,128]{2,1,0:T(8,128)S(1)}, u32[]{:S(2)}, u32[]{:S(2)}) collective-permute-start(f32[2,16,128]{2,1,0:T(8,128)S(1)} %get-tuple-element.190.refs_5_), channel_id=1, source_target_pairs={{0,6},{1,7},{2,4},{3,5},{4,2},{5,3},{6,0},{7,1},{8,14},{9,15},{10,... | collective-permute-start | bytes 49160 | tf_op jit(solution)/shard_map/cond/branch_1_fun/ppermute | solution.py:421
  111.5 21.3 %collective-permute-start.10 = (bf16[4,128,512]{2,1,0:T(8,128)(2,1)}, bf16[4,128,512]{2,1,0:T(8,128)(2,1)S(1)}, u32[]{:S(2)}, u32[]{:S(2)}) collective-permute-start(bf16[4,128,512]{2,1,0:T(8,128)(2,1)} %get-tuple-element.201), channel_id=1, source_target_pairs={{0,2},{1,3},{2,0},{3,1},{4,6},{5,7},{6,4},{7,5},{8,10},{9,11},{10,... | collective-permute-start | bytes 1572872 | tf_op jit(solution)/shard_map/cond/branch_1_fun/ppermute | solution.py:421
  116.7 23.3 %collective-permute-start.11 = (bf16[4,128,512]{2,1,0:T(8,128)(2,1)S(1)}, bf16[4,128,512]{2,1,0:T(8,128)(2,1)S(1)}, u32[]{:S(2)}, u32[]{:S(2)}) collective-permute-start(bf16[4,128,512]{2,1,0:T(8,128)(2,1)S(1)} %add_convert_fusion), channel_id=1, source_target_pairs={{0,4},{1,5},{2,6},{3,7},{4,0},{5,1},{6,2},{7,3},{8,12},{9,13},{10,... | collective-permute-start | bytes 1572872 | tf_op jit(solution)/shard_map/cond/branch_1_fun/ppermute | solution.py:421
  140.4 15.0 %collective-permute-start.21 = (bf16[4,128,512]{2,1,0:T(8,128)(2,1)}, bf16[4,128,512]{2,1,0:T(8,128)(2,1)S(1)}, u32[]{:S(2)}, u32[]{:S(2)}) collective-permute-start(bf16[4,128,512]{2,1,0:T(8,128)(2,1)} %get-tuple-element.274), channel_id=1, source_target_pairs={{0,2},{1,3},{2,0},{3,1},{4,6},{5,7},{6,4},{7,5},{8,10},{9,11},{10,... | collective-permute-start | bytes 1572872 | tf_op jit(solution)/shard_map/ppermute | solution.py:421
  146.5 19.6 %collective-permute-start.25 = (bf16[2,12,128,128]{3,2,1,0:T(8,128)(2,1)S(1)}, bf16[2,12,128,128]{3,2,1,0:T(8,128)(2,1)S(1)}, u32[]{:S(2)}, u32[]{:S(2)}) collective-permute-start(bf16[2,12,128,128]{3,2,1,0:T(8,128)(2,1)S(1)} %fusion.23), channel_id=1, source_target_pairs={{0,16},{8,24},{16,0},{24,8},{1,17},{9,25},{17,1},{25,9},{2,18},{10... | collective-permute-start | bytes 2359304 | tf_op jit(solution)/shard_map/ppermute | solution.py:427
  148.3 19.4 %collective-permute-start.24 = (bf16[2,12,128,128]{3,2,1,0:T(8,128)(2,1)S(1)}, bf16[2,12,128,128]{3,2,1,0:T(8,128)(2,1)S(1)}, u32[]{:S(2)}, u32[]{:S(2)}) collective-permute-start(bf16[2,12,128,128]{3,2,1,0:T(8,128)(2,1)S(1)} %fusion.22), channel_id=1, source_target_pairs={{0,1},{1,0},{2,3},{3,2},{4,5},{5,4},{6,7},{7,6},{8,9},{9,8},{10,11... | collective-permute-start | bytes 2359304 | tf_op jit(solution)/shard_map/ppermute | solution.py:424
  149.5 23.5 %collective-permute-start.20 = (bf16[4,128,512]{2,1,0:T(8,128)(2,1)S(1)}, bf16[4,128,512]{2,1,0:T(8,128)(2,1)S(1)}, u32[]{:S(2)}, u32[]{:S(2)}) collective-permute-start(bf16[4,128,512]{2,1,0:T(8,128)(2,1)S(1)} %copy-done.6), channel_id=1, source_target_pairs={{0,2},{1,3},{2,0},{3,1},{4,6},{5,7},{6,4},{7,5},{8,10},{9,11},{10,... | collective-permute-start | bytes 1572872 | tf_op jit(solution)/shard_map/ppermute | solution.py:421
  155.6 25.3 %collective-permute-start.23 = (bf16[4,128,512]{2,1,0:T(8,128)(2,1)S(1)}, bf16[4,128,512]{2,1,0:T(8,128)(2,1)S(1)}, u32[]{:S(2)}, u32[]{:S(2)}) collective-permute-start(bf16[4,128,512]{2,1,0:T(8,128)(2,1)S(1)} %add_convert_fusion.3), channel_id=1, source_target_pairs={{0,4},{1,5},{2,6},{3,7},{4,0},{5,1},{6,2},{7,3},{8,12},{9,13},{10,... | collective-permute-start | bytes 1572872 | tf_op jit(solution)/shard_map/ppermute | solution.py:421
  168.1 12.8 %collective-permute-start.26 = (bf16[12,128,128]{2,1,0:T(8,128)(2,1)S(1)}, bf16[12,128,128]{2,1,0:T(8,128)(2,1)S(1)}, u32[]{:S(2)}, u32[]{:S(2)}) collective-permute-start(bf16[12,128,128]{2,1,0:T(8,128)(2,1)S(1)} %get-tuple-element.308), channel_id=1, source_target_pairs={{0,16},{8,24},{16,0},{24,8},{1,17},{9,25},{17,1},{25,9},{2,18},{10... | collective-permute-start | bytes 1179656 | tf_op jit(solution)/shard_map/ppermute | solution.py:427
  169.2 11.6 %collective-permute-start.27 = (bf16[12,128,128]{2,1,0:T(8,128)(2,1)S(1)}, bf16[12,128,128]{2,1,0:T(8,128)(2,1)S(1)}, u32[]{:S(2)}, u32[]{:S(2)}) collective-permute-start(bf16[12,128,128]{2,1,0:T(8,128)(2,1)S(1)} %get-tuple-element.307), channel_id=1, source_target_pairs={{0,1},{1,0},{2,3},{3,2},{4,5},{5,4},{6,7},{7,6},{8,9},{9,8},{10,11... | collective-permute-start | bytes 1179656 | tf_op jit(solution)/shard_map/ppermute | solution.py:424
  (14 other events, 108.0 us)

commit v2 on v1

--- a/solution.py
+++ b/solution.py
@@ -436,16 +436,18 @@
         def moves(first, lists, table, core):
             half = table.shape[0] // 2
             sent = lax.dynamic_slice_in_dim(table, core * half, half, axis=0)
-            far, near, from_x = lax.optimization_barrier(
-                (self.over_z(first, 2), self.over_z(first, 1), self.over_x(sent))
-            )
-            return (near, far, self.over_z(far, 1)), (from_x, self.over_core(from_x)), prepare(
+            from_x = self.over_x(sent)
+            far, near = lax.optimization_barrier((self.over_z(first, 2), self.over_z(first, 1)))
+            return (near, far, self.over_z(far, 1)), from_x, prepare(
                 jnp.stack(self.all_over_z(lists))
             )
 
         first, second = chunks
-        pieces, tables, prepared = self.together(needed, moves, first, lists, table, core)
-        return [[first, *pieces], [second]], [table, *tables], prepared
+        pieces, from_x, prepared = self.together(needed, moves, first, lists, table, core)
+        return [[first, *pieces], [second]], [table, from_x], prepared
+
+    def all_tables(self, tables):
+        return [*tables, self.over_core(tables[-1])]
 
     def rest_of_rows(self, pieces, others):
         second, = pieces
@@ -521,6 +523,9 @@
     def gather(self, needed, chunks, lists, table, core, prepare):
         gathered = [[lax.all_gather(rows, "cls", tiled=True)] for rows in chunks]
         return gathered, [table], prepare(lax.all_gather(lists, "cls"))
+
+    def all_tables(self, tables):
+        return tables
 
     def rest_of_rows(self, pieces, others):
         return (), others
@@ -625,8 +630,9 @@
         parts, unit = score(held[chunk], *prepared[chunk], rows, tables)
         return moves.gather_stats(parts), unit
 
-    def early_work(gathered, tables, prepared):
+    def early_work(gathered, own_tables, prepared):
         units, made, rest = [], [], ()
+        tables = moves.all_tables(own_tables)
         for chunk in range(last):
             stats, unit = scored(chunk, gathered[chunk], tables, prepared)
             if chunk == 0:
@@ -636,7 +642,7 @@
                 held[chunk], *prepared[chunk], stats, moves.turned, unit, tables,
                 moves.grad_shapes(sizes[chunk]),
             ))
-        return rest, units, made
+        return rest, tables[len(own_tables):], units, made
 
     def last_work(rows, tables, prepared, units, scores, early):
         codes, metas, hits = zip(*prepared)
@@ -647,7 +653,8 @@
             moves.grad_shapes(sizes[-1]), moves.share_shapes(shard_tiles),
         )
 
-    rest, units, made = moves.together(needed, early_work, gathered, tables, prepared)
+    rest, more, units, made = moves.together(needed, early_work, gathered, tables, prepared)
+    tables = [*tables, *more]
     rows = moves.whole_rows(gathered[-1], rest)
     early, scores, losses = zip(*made)
     returned, (parts, shares, loss) = moves.together(
@@ -665,10 +672,14 @@
     unit_exact = emb_exact * inverse_norm
     proxy_grad = shares.reshape(shard_tiles * TILE, D // dp)
     row_loss = jnp.concatenate(losses, axis=0).reshape(-1)
-    grad_flat = jnp.concatenate(row_grads, axis=0)
-    grad_flat = grad_flat.reshape(blocks * BR, D)
-    radial = jnp.sum(unit_exact * grad_flat, axis=1, keepdims=True)
-    embed_grad = ((grad_flat - unit_exact * radial) * inverse_norm).astype(jnp.bfloat16)
+    embed_grad = []
+    for spot, grad_rows in zip(spots, row_grads):
+        span = slice(spot.start * BR, spot.stop * BR)
+        exact, norm = unit_exact[span], inverse_norm[span]
+        grad_rows = grad_rows.reshape(-1, D)
+        radial = jnp.sum(exact * grad_rows, axis=1, keepdims=True)
+        embed_grad.append(((grad_rows - exact * radial) * norm).astype(jnp.bfloat16))
+    embed_grad = jnp.concatenate(embed_grad, axis=0)
     return (row_loss, embed_grad, proxy_grad)
 
 

time: 185 us -> 174 us (0.941)
  waiting for transfers between devices: 96.1 us -> 81.6 us
    ppermute x21, waiting for transfers between devices: 73.3 us -> 64.6 us  [over_z(): return lax.ppermute(value, 'cls', pairs)]
    ppermute x3, waiting for transfers between devices: 6.51 us -> 3.47 us  [over_x(): lax.ppermute(value, 'cls', [(c, c ^ 1) for c in range(self.nx * self.nz)])]
    ppermute x21, starting transfers between devices: 26.1 us -> 29.1 us  [over_z(): return lax.ppermute(value, 'cls', pairs)]
  transfers between devices with their start and end apart: 28 -> 28, of which waited for: 17 -> 17; matrix products, arithmetic and copies ran while one was open for 4% -> 5% of each run, Pallas kernels for 20% -> 23%
where the time goes in v2:
time: 174 us
  waiting for transfers between devices  81.6 us (47%)
  Pallas kernels  39.2 us (23%)
  starting transfers between devices  36.2 us (21%)
  other arithmetic  11.1 us (6%)
  local copies, waits for them, and re-layouts  4.78 us (3%)
    ppermute x21, waiting for transfers between devices, over_z(): return lax.ppermute(value, 'cls', pairs)  64.6 us
    ppermute x21, starting transfers between devices, over_z(): return lax.ppermute(value, 'cls', pairs)  29.1 us
    pallas_call x2, Pallas kernels, score(): pl.pallas_call(functools.partial(score_kernel, len(rows), len(tables), bl...  15.7 us
    pallas_call x1, Pallas kernels, last_grads(): pl.pallas_call(functools.partial(last_kernel, sizes, len(shapes), len(tab...  14 us
    ppermute x2, waiting for transfers between devices, over_y(): return lax.ppermute(value, 'dp', [(d, d ^ 2) for d in range(self.dp)])  9.5 us
    pallas_call x1, Pallas kernels, grads(): pl.pallas_call(functools.partial(grad_kernel, len(shapes), len(tables), l...  9.44 us
    ppermute x3, starting transfers between devices, over_x(): lax.ppermute(value, 'cls', [(c, c ^ 1) for c in range(self.nx * self.nz)])  4.86 us
    ppermute x2, waiting for transfers between devices, over_core(): return lax.ppermute(value, 'dp', [(d, d ^ 1) for d in range(self.dp)])  4.07 us
  transfers between devices with their start and end apart: 28, of which 17 were waited for; matrix products, arithmetic and copies ran while one was open for 5% of the time, Pallas kernels for 23%

profile of v2, /device:TPU:0, one launch (start us, length us, event | category | flops | bytes accessed | tf_op | source)
XLA Modules:
  0.0 174.1 jit_solution(10393400669493244582)
XLA Ops:
  2.4 46.5 %conditional.3 = (bf16[4,128,512]{2,1,0:T(8,128)(2,1)}, bf16[4,128,512]{2,1,0:T(8,128)(2,1)}, bf16[4,128,512]{2,1,0:T(8,128)(2,1)}, bf16[12,128,512]{2,1,0:T(8,1...) conditional(s32[]{:T(128)} %bitcast.8, () %tuple.75, ...), branch_computations={%region_0.1_spmd, %region_1.8_spmd} | conditional | flops 232492 | bytes 15938830 | solution.py:489
  2.4 3.0 %collective-permute-start.17 = (s32[8,136]{1,0:T(8,128)S(1)}, s32[8,136]{1,0:T(8,128)S(1)}, u32[]{:S(2)}, u32[]{:S(2)}) collective-permute-start(s32[8,136]{1,0:T(8,128)S(1)} %get-tuple-element.145), channel_id=1, source_target_pairs={{0,2},{1,3},{2,0},{3,1},{4,6},{5,7},{6,4},{7,5},{8,10},{9,11},{10,... | collective-permute-start | bytes 13064 | tf_op jit(solution)/shard_map/cond/branch_1_fun/ppermute | solution.py:421
  5.4 2.6 %collective-permute-start.18 = (s32[8,136]{1,0:T(8,128)S(1)}, s32[8,136]{1,0:T(8,128)S(1)}, u32[]{:S(2)}, u32[]{:S(2)}) collective-permute-start(s32[8,136]{1,0:T(8,128)S(1)} %get-tuple-element.145), channel_id=1, source_target_pairs={{0,4},{1,5},{2,6},{3,7},{4,0},{5,1},{6,2},{7,3},{8,12},{9,13},{10,... | collective-permute-start | bytes 13064 | tf_op jit(solution)/shard_map/cond/branch_1_fun/ppermute | solution.py:421
  9.9 2.5 %collective-permute-start.14 = (bf16[4,128,512]{2,1,0:T(8,128)(2,1)S(1)}, bf16[4,128,512]{2,1,0:T(8,128)(2,1)}, u32[]{:S(2)}, u32[]{:S(2)}) collective-permute-start(bf16[4,128,512]{2,1,0:T(8,128)(2,1)S(1)} %get-tuple-element.140), channel_id=1, source_target_pairs={{0,2},{1,3},{2,0},{3,1},{4,6},{5,7},{6,4},{7,5},{8,10},{9,11},{10,... | collective-permute-start | bytes 1572872 | tf_op jit(solution)/shard_map/cond/branch_1_fun/ppermute | solution.py:421
  18.5 15.2 %collective-permute-done.13 = bf16[4,128,512]{2,1,0:T(8,128)(2,1)} collective-permute-done((bf16[4,128,512]{2,1,0:T(8,128)(2,1)S(1)}, bf16[4,128,512]{2,1,0:T(8,128)(2,1)}, u32[]{:S(2)}, u32[]{:S(2)}) %collective-permute-start.13) | collective-permute-done | bytes 524320 | tf_op jit(solution)/shard_map/cond/branch_1_fun/ppermute | solution.py:421
  35.0 11.9 %collective-permute-done.15 = bf16[4,128,512]{2,1,0:T(8,128)(2,1)} collective-permute-done((bf16[4,128,512]{2,1,0:T(8,128)(2,1)}, bf16[4,128,512]{2,1,0:T(8,128)(2,1)}, u32[]{:S(2)}, u32[]{:S(2)}) %collective-permute-start.15) | collective-permute-done | bytes 524320 | tf_op jit(solution)/shard_map/cond/branch_1_fun/ppermute | solution.py:421
  48.9 41.1 %conditional.4 = (bf16[4,128,512]{2,1,0:T(8,128)(2,1)}, bf16[4,128,512]{2,1,0:T(8,128)(2,1)}, bf16[4,128,512]{2,1,0:T(8,128)(2,1)}, bf16[12,128,512]{2,1,0:T(8,1...) conditional(s32[]{:T(128)} %bitcast.8, () %tuple.74, ...), branch_computations={%region_8.9_spmd, %region_9.10_spmd} | conditional | flops 2359296 | bytes 29036940 | solution.py:489
  52.6 8.3 %branch_1_fun.4 = (f32[2,16,128]{2,1,0:T(8,128)S(1)}, bf16[16,128,512]{2,1,0:T(8,128)(2,1)}) custom-call(s32[64]{0:T(128)S(1)} %get-tuple-element.149.codes_ref, s32[3]{0:T(128)S(1)} %get-tuple-element.150.meta_ref, s32[16,128]{1,0:T(8,128)S(1)} %get-tuple-element.151.hit_ref, bf16[4,128,512]{2,1,0:T(8,128)(2,1)S(1)} %get-tuple-element.152.refs_0_, ...), custom_call_target="tpu_custom_call" | custom-call | flops 1048576 | bytes 1048576 | tf_op jit(solution)/shard_map/cond/branch_1_fun/pallas_call | solution.py:315
  62.2 3.2 %collective-permute-start.5 = (f32[2,16,128]{2,1,0:T(8,128)S(1)}, f32[2,16,128]{2,1,0:T(8,128)S(1)}, u32[]{:S(2)}, u32[]{:S(2)}) collective-permute-start(f32[2,16,128]{2,1,0:T(8,128)S(1)} %get-tuple-element.162.refs_0_), channel_id=1, source_target_pairs={{0,6},{1,7},{2,4},{3,5},{4,2},{5,3},{6,0},{7,1},{8,14},{9,15},{10,... | collective-permute-start | bytes 49160 | tf_op jit(solution)/shard_map/cond/branch_1_fun/ppermute | solution.py:421
  65.5 9.9 %collective-permute-done = bf16[4,128,512]{2,1,0:T(8,128)(2,1)} collective-permute-done((bf16[4,128,512]{2,1,0:T(8,128)(2,1)S(1)}, bf16[4,128,512]{2,1,0:T(8,128)(2,1)}, u32[]{:S(2)}, u32[]{:S(2)}) %collective-permute-start) | collective-permute-done | bytes 524320 | tf_op jit(solution)/shard_map/cond/branch_1_fun/ppermute | solution.py:421
  77.1 9.4 %branch_1_fun.5 = (bf16[4,128,512]{2,1,0:T(8,128)(2,1)S(1)}, bf16[4,128,512]{2,1,0:T(8,128)(2,1)}, bf16[4,128,512]{2,1,0:T(8,128)(2,1)S(1)}, bf16[4,128,512]{2,1...) custom-call(s32[64]{0:T(128)S(1)} %get-tuple-element.149.codes_ref, ...), custom_call_target="tpu_custom_call" | custom-call | flops 1048576 | bytes 1048576 | tf_op jit(solution)/shard_map/cond/branch_1_fun/pallas_call | solution.py:339
  86.7 3.4 %collective-permute-done.6 = bf16[4,128,512]{2,1,0:T(8,128)(2,1)} collective-permute-done((bf16[4,128,512]{2,1,0:T(8,128)(2,1)}, bf16[4,128,512]{2,1,0:T(8,128)(2,1)}, u32[]{:S(2)}, u32[]{:S(2)}) %collective-permute-start.6) | collective-permute-done | bytes 524320 | tf_op jit(solution)/shard_map/cond/branch_1_fun/ppermute | solution.py:421
  91.0 38.9 %conditional.5 = (bf16[4,128,512]{2,1,0:T(8,128)(2,1)}, bf16[4,128,512]{2,1,0:T(8,128)(2,1)}, bf16[2,2,24,128,128]{4,3,2,1,0:T(8,128)(2,1)S(1)}, bf16[2,2,24,128...) conditional(s32[]{:T(128)} %bitcast.8, () %tuple.78, ...), branch_computations={%region_10.11_spmd, %region_11.12_spmd} | conditional | flops 5242880 | bytes 38474096 | solution.py:489
  92.3 7.4 %branch_1_fun.6 = (f32[2,16,128]{2,1,0:T(8,128)S(1)}, bf16[16,128,512]{2,1,0:T(8,128)(2,1)S(1)}) custom-call(s32[64]{0:T(128)S(1)} %get-tuple-element.173.codes_ref.refs_1_, s32[3]{0:T(128)S(1)} %get-tuple-element.175.meta_ref.refs_3_, s32[16,128]{1,0:T(8,128)S(1)} %get-tuple-element.176.hit_ref.refs_4_, ...), custom_call_target="tpu_custom_call" | custom-call | flops 1048576 | bytes 1048576 | tf_op jit(solution)/shard_map/cond/branch_1_fun/pallas_call | solution.py:315
  101.6 2.5 %collective-permute-start.9 = (f32[2,16,128]{2,1,0:T(8,128)S(1)}, f32[2,16,128]{2,1,0:T(8,128)S(1)}, u32[]{:S(2)}, u32[]{:S(2)}) collective-permute-start(f32[2,16,128]{2,1,0:T(8,128)S(1)} %get-tuple-element.186.refs_5_), channel_id=1, source_target_pairs={{0,4},{1,5},{2,6},{3,7},{4,0},{5,1},{6,2},{7,3},{8,12},{9,13},{10,... | collective-permute-start | bytes 49160 | tf_op jit(solution)/shard_map/cond/branch_1_fun/ppermute | solution.py:421
  104.1 2.4 %collective-permute-done.10.refs_8_ = f32[2,16,128]{2,1,0:T(8,128)S(1)} collective-permute-done((f32[2,16,128]{2,1,0:T(8,128)S(1)}, f32[2,16,128]{2,1,0:T(8,128)S(1)}, u32[]{:S(2)}, u32[]{:S(2)}) %collective-permute-start.10) | collective-permute-done | bytes 16416 | tf_op jit(solution)/shard_map/cond/branch_1_fun/ppermute | solution.py:421
  106.7 2.5 %collective-permute-start.12 = (bf16[4,128,512]{2,1,0:T(8,128)(2,1)S(1)}, bf16[4,128,512]{2,1,0:T(8,128)(2,1)S(1)}, u32[]{:S(2)}, u32[]{:S(2)}) collective-permute-start(bf16[4,128,512]{2,1,0:T(8,128)(2,1)S(1)} %add_convert_fusion), channel_id=1, source_target_pairs={{0,4},{1,5},{2,6},{3,7},{4,0},{5,1},{6,2},{7,3},{8,12},{9,13},{10,... | collective-permute-start | bytes 1572872 | tf_op jit(solution)/shard_map/cond/branch_1_fun/ppermute | solution.py:421
  109.2 14.0 %branch_1_fun.7 = (bf16[4,128,512]{2,1,0:T(8,128)(2,1)S(1)}, bf16[4,128,512]{2,1,0:T(8,128)(2,1)}, bf16[4,128,512]{2,1,0:T(8,128)(2,1)S(1)}, bf16[4,128,512]{2,1...) custom-call(s32[64]{0:T(128)S(1)} %get-tuple-element.172.refs_0_, ...), custom_call_target="tpu_custom_call" | custom-call | flops 2097152 | bytes 2097152 | tf_op jit(solution)/shard_map/cond/branch_1_fun/pallas_call | solution.py:374
  123.5 2.9 %collective-permute-done.11 = bf16[4,128,512]{2,1,0:T(8,128)(2,1)S(1)} collective-permute-done((bf16[4,128,512]{2,1,0:T(8,128)(2,1)}, bf16[4,128,512]{2,1,0:T(8,128)(2,1)S(1)}, u32[]{:S(2)}, u32[]{:S(2)}) %collective-permute-start.11) | collective-permute-done | bytes 524320 | tf_op jit(solution)/shard_map/cond/branch_1_fun/ppermute | solution.py:421
  126.6 3.0 %collective-permute-done.12 = bf16[4,128,512]{2,1,0:T(8,128)(2,1)S(1)} collective-permute-done((bf16[4,128,512]{2,1,0:T(8,128)(2,1)S(1)}, bf16[4,128,512]{2,1,0:T(8,128)(2,1)S(1)}, u32[]{:S(2)}, u32[]{:S(2)}) %collective-permute-start.12) | collective-permute-done | bytes 524320 | tf_op jit(solution)/shard_map/cond/branch_1_fun/ppermute | solution.py:421
  139.9 5.1 %collective-permute-done.21 = bf16[4,128,512]{2,1,0:T(8,128)(2,1)S(1)} collective-permute-done((bf16[4,128,512]{2,1,0:T(8,128)(2,1)}, bf16[4,128,512]{2,1,0:T(8,128)(2,1)S(1)}, u32[]{:S(2)}, u32[]{:S(2)}) %collective-permute-start.21) | collective-permute-done | bytes 524320 | tf_op jit(solution)/shard_map/ppermute | solution.py:421
  146.2 9.5 %collective-permute-done.25 = bf16[2,12,128,128]{3,2,1,0:T(8,128)(2,1)S(1)} collective-permute-done((bf16[2,12,128,128]{3,2,1,0:T(8,128)(2,1)S(1)}, bf16[2,12,128,128]{3,2,1,0:T(8,128)(2,1)S(1)}, u32[]{:S(2)}, u32[]{:S(2)}) %collective-permute-start.25) | collective-permute-done | bytes 786464 | tf_op jit(solution)/shard_map/ppermute | solution.py:427
  160.7 3.5 %collective-permute-done.20 = bf16[4,128,512]{2,1,0:T(8,128)(2,1)S(1)} collective-permute-done((bf16[4,128,512]{2,1,0:T(8,128)(2,1)}, bf16[4,128,512]{2,1,0:T(8,128)(2,1)S(1)}, u32[]{:S(2)}, u32[]{:S(2)}) %collective-permute-start.20) | collective-permute-done | bytes 524320 | tf_op jit(solution)/shard_map/ppermute | solution.py:421
  164.2 6.3 %collective-permute-done.23 = bf16[4,128,512]{2,1,0:T(8,128)(2,1)S(1)} collective-permute-done((bf16[4,128,512]{2,1,0:T(8,128)(2,1)S(1)}, bf16[4,128,512]{2,1,0:T(8,128)(2,1)S(1)}, u32[]{:S(2)}, u32[]{:S(2)}) %collective-permute-start.23) | collective-permute-done | bytes 524320 | tf_op jit(solution)/shard_map/ppermute | solution.py:421
  (114 shorter events, 44.2 us)
Async XLA Ops:
  2.4 11.6 %collective-permute-start.17 = (s32[8,136]{1,0:T(8,128)S(1)}, s32[8,136]{1,0:T(8,128)S(1)}, u32[]{:S(2)}, u32[]{:S(2)}) collective-permute-start(s32[8,136]{1,0:T(8,128)S(1)} %get-tuple-element.145), channel_id=1, source_target_pairs={{0,2},{1,3},{2,0},{3,1},{4,6},{5,7},{6,4},{7,5},{8,10},{9,11},{10,... | collective-permute-start | bytes 13064 | tf_op jit(solution)/shard_map/cond/branch_1_fun/ppermute | solution.py:421
  5.4 10.2 %collective-permute-start.18 = (s32[8,136]{1,0:T(8,128)S(1)}, s32[8,136]{1,0:T(8,128)S(1)}, u32[]{:S(2)}, u32[]{:S(2)}) collective-permute-start(s32[8,136]{1,0:T(8,128)S(1)} %get-tuple-element.145), channel_id=1, source_target_pairs={{0,4},{1,5},{2,6},{3,7},{4,0},{5,1},{6,2},{7,3},{8,12},{9,13},{10,... | collective-permute-start | bytes 13064 | tf_op jit(solution)/shard_map/cond/branch_1_fun/ppermute | solution.py:421
  8.0 7.6 %collective-permute-start.19 = (s32[8,136]{1,0:T(8,128)S(1)}, s32[8,136]{1,0:T(8,128)S(1)}, u32[]{:S(2)}, u32[]{:S(2)}) collective-permute-start(s32[8,136]{1,0:T(8,128)S(1)} %get-tuple-element.145), channel_id=1, source_target_pairs={{0,6},{1,7},{2,4},{3,5},{4,2},{5,3},{6,0},{7,1},{8,14},{9,15},{10,... | collective-permute-start | bytes 13064 | tf_op jit(solution)/shard_map/cond/branch_1_fun/ppermute | solution.py:421
  8.0 25.7 %collective-permute-start.13 = (bf16[4,128,512]{2,1,0:T(8,128)(2,1)S(1)}, bf16[4,128,512]{2,1,0:T(8,128)(2,1)}, u32[]{:S(2)}, u32[]{:S(2)}) collective-permute-start(bf16[4,128,512]{2,1,0:T(8,128)(2,1)S(1)} %get-tuple-element.140), channel_id=1, source_target_pairs={{0,4},{1,5},{2,6},{3,7},{4,0},{5,1},{6,2},{7,3},{8,12},{9,13},{10,... | collective-permute-start | bytes 1572872 | tf_op jit(solution)/shard_map/cond/branch_1_fun/ppermute | solution.py:421
  9.9 23.8 %collective-permute-start.14 = (bf16[4,128,512]{2,1,0:T(8,128)(2,1)S(1)}, bf16[4,128,512]{2,1,0:T(8,128)(2,1)}, u32[]{:S(2)}, u32[]{:S(2)}) collective-permute-start(bf16[4,128,512]{2,1,0:T(8,128)(2,1)S(1)} %get-tuple-element.140), channel_id=1, source_target_pairs={{0,2},{1,3},{2,0},{3,1},{4,6},{5,7},{6,4},{7,5},{8,10},{9,11},{10,... | collective-permute-start | bytes 1572872 | tf_op jit(solution)/shard_map/cond/branch_1_fun/ppermute | solution.py:421
  14.0 34.9 %collective-permute-start.16 = (bf16[12,128,512]{2,1,0:T(8,128)(2,1)S(1)}, bf16[12,128,512]{2,1,0:T(8,128)(2,1)}, u32[]{:S(2)}, u32[]{:S(2)}) collective-permute-start(bf16[12,128,512]{2,1,0:T(8,128)(2,1)S(1)} %constant_dynamic-slice_fusion), channel_id=1, source_target_pairs={{0,1},{1,0},{2,3},{3,2},{4,5},{5,4},{6,7},{7,6},{8,9},{9,8},{10,11... | collective-permute-start | bytes 4718600 | tf_op jit(solution)/shard_map/cond/branch_1_fun/ppermute | solution.py:424
  33.7 13.2 %collective-permute-start.15 = (bf16[4,128,512]{2,1,0:T(8,128)(2,1)}, bf16[4,128,512]{2,1,0:T(8,128)(2,1)}, u32[]{:S(2)}, u32[]{:S(2)}) collective-permute-start(bf16[4,128,512]{2,1,0:T(8,128)(2,1)} %collective-permute-done.13), channel_id=1, source_target_pairs={{0,2},{1,3},{2,0},{3,1},{4,6},{5,7},{6,4},{7,5},{8,10},{9,11},{10,... | collective-permute-start | bytes 1572872 | tf_op jit(solution)/shard_map/cond/branch_1_fun/ppermute | solution.py:421
  48.9 26.4 %collective-permute-start = (bf16[4,128,512]{2,1,0:T(8,128)(2,1)S(1)}, bf16[4,128,512]{2,1,0:T(8,128)(2,1)}, u32[]{:S(2)}, u32[]{:S(2)}) collective-permute-start(bf16[4,128,512]{2,1,0:T(8,128)(2,1)S(1)} %get-tuple-element.148), channel_id=1, source_target_pairs={{0,4},{1,5},{2,6},{3,7},{4,0},{5,1},{6,2},{7,3},{8,12},{9,13},{10,... | collective-permute-start | bytes 1572872 | tf_op jit(solution)/shard_map/cond/branch_1_fun/ppermute | solution.py:421
  49.2 26.2 %collective-permute-start.1 = (bf16[4,128,512]{2,1,0:T(8,128)(2,1)S(1)}, bf16[4,128,512]{2,1,0:T(8,128)(2,1)}, u32[]{:S(2)}, u32[]{:S(2)}) collective-permute-start(bf16[4,128,512]{2,1,0:T(8,128)(2,1)S(1)} %get-tuple-element.148), channel_id=1, source_target_pairs={{0,2},{1,3},{2,0},{3,1},{4,6},{5,7},{6,4},{7,5},{8,10},{9,11},{10,... | collective-permute-start | bytes 1572872 | tf_op jit(solution)/shard_map/cond/branch_1_fun/ppermute | solution.py:421
  61.0 14.9 %collective-permute-start.3 = (f32[2,16,128]{2,1,0:T(8,128)S(1)}, f32[2,16,128]{2,1,0:T(8,128)S(1)}, u32[]{:S(2)}, u32[]{:S(2)}) collective-permute-start(f32[2,16,128]{2,1,0:T(8,128)S(1)} %get-tuple-element.162.refs_0_), channel_id=1, source_target_pairs={{0,2},{1,3},{2,0},{3,1},{4,6},{5,7},{6,4},{7,5},{8,10},{9,11},{10,... | collective-permute-start | bytes 49160 | tf_op jit(solution)/shard_map/cond/branch_1_fun/ppermute | solution.py:421
  61.3 14.6 %collective-permute-start.4 = (f32[2,16,128]{2,1,0:T(8,128)S(1)}, f32[2,16,128]{2,1,0:T(8,128)S(1)}, u32[]{:S(2)}, u32[]{:S(2)}) collective-permute-start(f32[2,16,128]{2,1,0:T(8,128)S(1)} %get-tuple-element.162.refs_0_), channel_id=1, source_target_pairs={{0,4},{1,5},{2,6},{3,7},{4,0},{5,1},{6,2},{7,3},{8,12},{9,13},{10,... | collective-permute-start | bytes 49160 | tf_op jit(solution)/shard_map/cond/branch_1_fun/ppermute | solution.py:421
  62.2 14.1 %collective-permute-start.5 = (f32[2,16,128]{2,1,0:T(8,128)S(1)}, f32[2,16,128]{2,1,0:T(8,128)S(1)}, u32[]{:S(2)}, u32[]{:S(2)}) collective-permute-start(f32[2,16,128]{2,1,0:T(8,128)S(1)} %get-tuple-element.162.refs_0_), channel_id=1, source_target_pairs={{0,6},{1,7},{2,4},{3,5},{4,2},{5,3},{6,0},{7,1},{8,14},{9,15},{10,... | collective-permute-start | bytes 49160 | tf_op jit(solution)/shard_map/cond/branch_1_fun/ppermute | solution.py:421
  76.3 13.8 %collective-permute-start.6 = (bf16[4,128,512]{2,1,0:T(8,128)(2,1)}, bf16[4,128,512]{2,1,0:T(8,128)(2,1)}, u32[]{:S(2)}, u32[]{:S(2)}) collective-permute-start(bf16[4,128,512]{2,1,0:T(8,128)(2,1)} %collective-permute-done), channel_id=1, source_target_pairs={{0,2},{1,3},{2,0},{3,1},{4,6},{5,7},{6,4},{7,5},{8,10},{9,11},{10,... | collective-permute-start | bytes 1572872 | tf_op jit(solution)/shard_map/cond/branch_1_fun/ppermute | solution.py:421
  91.0 15.5 %collective-permute-start.7 = (bf16[4,128,512]{2,1,0:T(8,128)(2,1)S(1)}, bf16[4,128,512]{2,1,0:T(8,128)(2,1)S(1)}, u32[]{:S(2)}, u32[]{:S(2)}) collective-permute-start(bf16[4,128,512]{2,1,0:T(8,128)(2,1)S(1)} %get-tuple-element.177), channel_id=1, source_target_pairs={{0,2},{1,3},{2,0},{3,1},{4,6},{5,7},{6,4},{7,5},{8,10},{9,11},{10,... | collective-permute-start | bytes 1572872 | tf_op jit(solution)/shard_map/cond/branch_1_fun/ppermute | solution.py:421
  99.6 6.9 %collective-permute-start.10 = (f32[2,16,128]{2,1,0:T(8,128)S(1)}, f32[2,16,128]{2,1,0:T(8,128)S(1)}, u32[]{:S(2)}, u32[]{:S(2)}) collective-permute-start(f32[2,16,128]{2,1,0:T(8,128)S(1)} %get-tuple-element.186.refs_5_), channel_id=1, source_target_pairs={{0,6},{1,7},{2,4},{3,5},{4,2},{5,3},{6,0},{7,1},{8,14},{9,15},{10,... | collective-permute-start | bytes 49160 | tf_op jit(solution)/shard_map/cond/branch_1_fun/ppermute | solution.py:421
  104.1 22.3 %collective-permute-start.11 = (bf16[4,128,512]{2,1,0:T(8,128)(2,1)}, bf16[4,128,512]{2,1,0:T(8,128)(2,1)S(1)}, u32[]{:S(2)}, u32[]{:S(2)}) collective-permute-start(bf16[4,128,512]{2,1,0:T(8,128)(2,1)} %get-tuple-element.197), channel_id=1, source_target_pairs={{0,2},{1,3},{2,0},{3,1},{4,6},{5,7},{6,4},{7,5},{8,10},{9,11},{10,... | collective-permute-start | bytes 1572872 | tf_op jit(solution)/shard_map/cond/branch_1_fun/ppermute | solution.py:421
  106.7 22.9 %collective-permute-start.12 = (bf16[4,128,512]{2,1,0:T(8,128)(2,1)S(1)}, bf16[4,128,512]{2,1,0:T(8,128)(2,1)S(1)}, u32[]{:S(2)}, u32[]{:S(2)}) collective-permute-start(bf16[4,128,512]{2,1,0:T(8,128)(2,1)S(1)} %add_convert_fusion), channel_id=1, source_target_pairs={{0,4},{1,5},{2,6},{3,7},{4,0},{5,1},{6,2},{7,3},{8,12},{9,13},{10,... | collective-permute-start | bytes 1572872 | tf_op jit(solution)/shard_map/cond/branch_1_fun/ppermute | solution.py:421
  130.0 15.0 %collective-permute-start.21 = (bf16[4,128,512]{2,1,0:T(8,128)(2,1)}, bf16[4,128,512]{2,1,0:T(8,128)(2,1)S(1)}, u32[]{:S(2)}, u32[]{:S(2)}) collective-permute-start(bf16[4,128,512]{2,1,0:T(8,128)(2,1)} %get-tuple-element.271), channel_id=1, source_target_pairs={{0,2},{1,3},{2,0},{3,1},{4,6},{5,7},{6,4},{7,5},{8,10},{9,11},{10,... | collective-permute-start | bytes 1572872 | tf_op jit(solution)/shard_map/ppermute | solution.py:421
  130.1 34.2 %collective-permute-start.20 = (bf16[4,128,512]{2,1,0:T(8,128)(2,1)}, bf16[4,128,512]{2,1,0:T(8,128)(2,1)S(1)}, u32[]{:S(2)}, u32[]{:S(2)}) collective-permute-start(bf16[4,128,512]{2,1,0:T(8,128)(2,1)} %get-tuple-element.270), channel_id=1, source_target_pairs={{0,2},{1,3},{2,0},{3,1},{4,6},{5,7},{6,4},{7,5},{8,10},{9,11},{10,... | collective-permute-start | bytes 1572872 | tf_op jit(solution)/shard_map/ppermute | solution.py:421
  136.1 19.6 %collective-permute-start.25 = (bf16[2,12,128,128]{3,2,1,0:T(8,128)(2,1)S(1)}, bf16[2,12,128,128]{3,2,1,0:T(8,128)(2,1)S(1)}, u32[]{:S(2)}, u32[]{:S(2)}) collective-permute-start(bf16[2,12,128,128]{3,2,1,0:T(8,128)(2,1)S(1)} %fusion.23), channel_id=1, source_target_pairs={{0,16},{8,24},{16,0},{24,8},{1,17},{9,25},{17,1},{25,9},{2,18},{10... | collective-permute-start | bytes 2359304 | tf_op jit(solution)/shard_map/ppermute | solution.py:427
  137.9 19.4 %collective-permute-start.24 = (bf16[2,12,128,128]{3,2,1,0:T(8,128)(2,1)S(1)}, bf16[2,12,128,128]{3,2,1,0:T(8,128)(2,1)S(1)}, u32[]{:S(2)}, u32[]{:S(2)}) collective-permute-start(bf16[2,12,128,128]{3,2,1,0:T(8,128)(2,1)S(1)} %fusion.22), channel_id=1, source_target_pairs={{0,1},{1,0},{2,3},{3,2},{4,5},{5,4},{6,7},{7,6},{8,9},{9,8},{10,11... | collective-permute-start | bytes 2359304 | tf_op jit(solution)/shard_map/ppermute | solution.py:424
  145.2 25.3 %collective-permute-start.23 = (bf16[4,128,512]{2,1,0:T(8,128)(2,1)S(1)}, bf16[4,128,512]{2,1,0:T(8,128)(2,1)S(1)}, u32[]{:S(2)}, u32[]{:S(2)}) collective-permute-start(bf16[4,128,512]{2,1,0:T(8,128)(2,1)S(1)} %add_convert_fusion.3), channel_id=1, source_target_pairs={{0,4},{1,5},{2,6},{3,7},{4,0},{5,1},{6,2},{7,3},{8,12},{9,13},{10,... | collective-permute-start | bytes 1572872 | tf_op jit(solution)/shard_map/ppermute | solution.py:421
  157.6 12.9 %collective-permute-start.26 = (bf16[12,128,128]{2,1,0:T(8,128)(2,1)S(1)}, bf16[12,128,128]{2,1,0:T(8,128)(2,1)S(1)}, u32[]{:S(2)}, u32[]{:S(2)}) collective-permute-start(bf16[12,128,128]{2,1,0:T(8,128)(2,1)S(1)} %get-tuple-element.306), channel_id=1, source_target_pairs={{0,16},{8,24},{16,0},{24,8},{1,17},{9,25},{17,1},{25,9},{2,18},{10... | collective-permute-start | bytes 1179656 | tf_op jit(solution)/shard_map/ppermute | solution.py:427
  158.3 12.2 %collective-permute-start.27 = (bf16[12,128,128]{2,1,0:T(8,128)(2,1)S(1)}, bf16[12,128,128]{2,1,0:T(8,128)(2,1)S(1)}, u32[]{:S(2)}, u32[]{:S(2)}) collective-permute-start(bf16[12,128,128]{2,1,0:T(8,128)(2,1)S(1)} %get-tuple-element.305), channel_id=1, source_target_pairs={{0,1},{1,0},{2,3},{3,2},{4,5},{5,4},{6,7},{7,6},{8,9},{9,8},{10,11... | collective-permute-start | bytes 1179656 | tf_op jit(solution)/shard_map/ppermute | solution.py:424
  (13 other events, 102.2 us)
